TPU v7x, 32 devices: a whole 2x2x4 slice. The times are simulated.
32 devices in a mesh: grp: 2 (over x), xfer: 16 (over z, y, core).
Axes of the slice: x: 2, y: 2, z: 4, core: 2. Of those that a mesh axis runs over, the one named last changes fastest.
Arguments:
- cq: bfloat16 [128, 2, 1536], P(('grp', 'xfer')), parts along dimension 0, may hold values from -6 to 6
- new_kv: bfloat16 [128, 2, 576], P(('grp', 'xfer')), parts along dimension 0, may hold values from -12 to 12
- cache: bfloat16 [16, 4096, 576], P('grp', 'xfer'), parts along dimension 0, may hold values from -28 to 28
- prompt_len: int32 [16], P('grp'), parts along dimension 0, may hold values from 1024 to 4096, as said below
- prefill_owner: int32 [16], P('grp'), parts along dimension 0, may hold values from 0 to 15
- cand_req: int32 [128], P('grp'), parts along dimension 0, may hold values from 0 to 7, as said below
- w_q: bfloat16 [1536, 73728], P(None, 'xfer'), may hold values from -0.15625 to 0.15625
- value_up_weight: bfloat16 [128, 512, 128], P('xfer'), may hold values from -0.25 to 0.25
- w_o: bfloat16 [16384, 7168], P('xfer'), may hold values from -0.046875 to 0.046875
Outputs:
- out: bfloat16 [128, 2, 7168], P(('grp', 'xfer')), parts along dimension 0
There are 2 independent parts, one for each index of `grp`. A program takes and returns all parts, laid end to end along the dimension named above; an argument that names none is the same for every part. Nothing has to cross between parts.
Inputs may be any that keep to these rules, and one draw needn't show every extreme that they name: `prompt_len`: one prompt has exactly 4096 rows. `cand_req`: the 4 candidates of one device belong to one request, and devices 2k and 2k + 1 of the xfer axis hold the candidates of one request, which no other device holds.
All inputs are finite; a program needn't handle non-finite values.
Results may differ from a plain program's by a relative error of at most 0.0049.
The roundings to bfloat16 on the way count: a program that leaves them out, or rounds other values in their place, can miss the bound.
Values may be sent and summed in bfloat16 or wider, within the bound.
A program may use at most 128 MiB of HBM per device.

v0:
```python
import jax
import jax.numpy as jnp
from jax import lax
from jax.sharding import PartitionSpec as P

SCORE_SCALE = 0.135
key_block = 2048


def own_terms(queries_here, self_key_rows):
    step_count = queries_here.shape[2]
    step_index = jnp.arange(step_count, dtype=jnp.int32)
    causal = step_index[None, :] <= step_index[:, None]
    own_scores = (
        jnp.einsum(
            "gcshk,ctk->gcsht", queries_here, self_key_rows, preferred_element_type=jnp.float32
        )
        * SCORE_SCALE
    )
    own_scores = jnp.where(causal[None, None, :, None, :], own_scores, -jnp.inf)
    first_top = jnp.max(own_scores, axis=-1)
    first_sum = jnp.sum(jnp.exp(own_scores - first_top[..., None]), axis=-1)
    return (own_scores, first_top, first_sum)


def block_scores(queries_here, cached_key_rows, live_rows, block_number, block_width):
    block_keys = lax.dynamic_slice_in_dim(
        cached_key_rows, block_number * block_width, block_width, 0
    )
    block_live = lax.dynamic_slice_in_dim(live_rows, block_number * block_width, block_width, 0)
    scores = (
        jnp.einsum("gcshk,lk->gcshl", queries_here, block_keys, preferred_element_type=jnp.float32)
        * SCORE_SCALE
    )
    return (block_keys, jnp.where(block_live, scores, -jnp.inf))


def scan_stats(queries_here, cached_key_rows, live_rows, trip_count, block_width, initial):

    def statistics(block_number, carry):
        largest, denominator = carry
        _, scores = block_scores(
            queries_here, cached_key_rows, live_rows, block_number, block_width
        )
        new_largest = jnp.maximum(largest, jnp.max(scores, axis=-1))
        denominator = denominator * jnp.exp(largest - new_largest) + jnp.sum(
            jnp.exp(scores - new_largest[..., None]), axis=-1
        )
        return (new_largest, denominator)

    return lax.fori_loop(0, trip_count, statistics, initial)


def scan_latents(
    queries_here,
    cached_key_rows,
    live_rows,
    trip_count,
    block_width,
    largest,
    denominator,
    latent_width,
    initial,
):

    def accumulate(block_number, running):
        block_keys, scores = block_scores(
            queries_here, cached_key_rows, live_rows, block_number, block_width
        )
        weights = (jnp.exp(scores - largest[..., None]) / denominator[..., None]).astype(
            jnp.bfloat16
        )
        return running + jnp.einsum(
            "gcshl,lk->gcshk",
            weights,
            block_keys[:, :latent_width],
            preferred_element_type=jnp.float32,
        )

    return lax.fori_loop(0, trip_count, accumulate, initial)


def attend(
    queries_here, self_key_rows, cached_key_rows, live_rows, trip_count, block_width, latent_width
):
    own_scores, first_top, first_sum = own_terms(queries_here, self_key_rows)
    largest, denominator = scan_stats(
        queries_here, cached_key_rows, live_rows, trip_count, block_width, (first_top, first_sum)
    )
    self_prob_weights = (jnp.exp(own_scores - largest[..., None]) / denominator[..., None]).astype(
        jnp.bfloat16
    )
    initial = jnp.einsum(
        "gcsht,ctk->gcshk",
        self_prob_weights,
        self_key_rows[:, :, :latent_width],
        preferred_element_type=jnp.float32,
    )
    total = scan_latents(
        queries_here,
        cached_key_rows,
        live_rows,
        trip_count,
        block_width,
        largest,
        denominator,
        latent_width,
        initial,
    )
    return total.astype(jnp.bfloat16)


def shards(cq, new_kv, cache, prompt_len, prefill_owner, cand_req, w_q, value_up_weight, w_o):
    devices = lax.axis_size("xfer")
    device = lax.axis_index("xfer")
    cand_here, step_count, _ = cq.shape
    local_heads, latent_width, value_width = value_up_weight.shape
    segment = cache.shape[1]
    kv_width = cache.shape[2]
    length = segment * devices
    part_rows = lax.all_gather(cq, "xfer", axis=0, tiled=True)
    row_count = part_rows.shape[0]
    flat_rows = jnp.dot(
        part_rows.reshape(row_count * step_count, part_rows.shape[2]),
        w_q,
        preferred_element_type=jnp.float32,
    )
    head_queries = flat_rows.astype(jnp.bfloat16).reshape(row_count, step_count, w_q.shape[1])
    exchanged = lax.all_to_all(head_queries, "xfer", split_axis=0, concat_axis=0, tiled=True)
    queries_here = exchanged.reshape(devices, cand_here, step_count, local_heads, kv_width)
    dest_request = cand_req.reshape(devices, cand_here)[:, 0]
    outgoing = jnp.take(cache, dest_request, axis=0)
    my_request = lax.dynamic_index_in_dim(dest_request, device, 0, keepdims=False)
    my_length = lax.dynamic_index_in_dim(prompt_len, my_request, 0, keepdims=False)
    first_owner = lax.dynamic_index_in_dim(prefill_owner, my_request, 0, keepdims=False)
    incoming = lax.all_to_all(outgoing, "xfer", split_axis=0, concat_axis=0, tiled=True)
    cached_key_rows = incoming.reshape(length, kv_width)
    row_index = jnp.arange(length, dtype=jnp.int32)
    block_width = min(key_block, length)
    position = (row_index // segment - first_owner) % devices * segment + row_index % segment
    compressed_states = attend(
        queries_here,
        new_kv,
        cached_key_rows,
        position < my_length,
        length // block_width,
        block_width,
        latent_width,
    )
    returned = lax.all_to_all(compressed_states, "xfer", split_axis=0, concat_axis=0, tiled=True)
    per_head_latent = returned.reshape(cand_here * devices, step_count, local_heads, latent_width)
    per_head_value = jnp.einsum(
        "diwu,wut->diwt", per_head_latent, value_up_weight, preferred_element_type=jnp.float32
    )
    per_head_value = per_head_value.astype(jnp.bfloat16).reshape(
        cand_here * devices, step_count, local_heads * value_width
    )
    row_count = lax.axis_size("xfer") * cand_here
    flat_rows = jnp.dot(
        per_head_value.reshape(row_count * step_count, -1), w_o, preferred_element_type=jnp.float32
    )
    summed = lax.psum_scatter(
        flat_rows.reshape(row_count, step_count, w_o.shape[1]),
        "xfer",
        scatter_dimension=0,
        tiled=True,
    )
    return summed.astype(jnp.bfloat16)


def solution(mesh):
    in_specs = (
        P(("grp", "xfer"), None, None),
        P(("grp", "xfer"), None, None),
        P("grp", "xfer", None),
        P("grp"),
        P("grp"),
        P("grp"),
        P(None, "xfer"),
        P("xfer", None, None),
        P("xfer", None),
    )
    out_specs = P(("grp", "xfer"), None, None)
    return jax.shard_map(shards, mesh=mesh, in_specs=in_specs, out_specs=out_specs, check_vma=False)
```

profile of v0, /device:TPU:0, one launch (start us, length us, event | category | flops | bytes accessed | tf_op | source)
XLA Modules:
  0.0 342.0 jit_solution(4454631070632522112)
XLA Ops:
  0.0 24.5 %all_gather.3 = bf16[64,2,1536]{2,1,0:T(2,128)(2,1)S(1)} all-gather(bf16[4,2,1536]{2,1,0:T(2,128)(2,1)} %param.13), channel_id=1, replica_groups=mesh['grp'=2,'xfer'=16] {'xfer'}, dimensions={0}, use_global_device_ids=true | all-gather | bytes 417792 | tf_op jit(solution)/shard_map/all_gather | solution.py:121
  25.4 7.2 %convolution_convert_fusion = bf16[128,4608]{1,0:T(8,128)(2,1)S(1)} fusion(bf16[128,1536]{1,0:T(8,128)(2,1)} %reshape.45, bf16[1536,4608]{1,0:T(8,128)(2,1)} %param.19), kind=kOutput, calls=%fused_computation.24 | convolution fusion | flops 1812529152 | bytes 15728640 | tf_op jit(solution)/shard_map/dot_general | solution.py:123
  33.9 3.7 %all-to-all-start = ((bf16[64,2,4608]{2,1,0:T(2,128)(2,1)}), bf16[64,2,4608]{2,1,0:T(2,128)(2,1)S(1)}, u32[]{:S(2)}, u32[]{:S(2)}) async-start(bf16[64,2,4608]{2,1,0:T(2,128)(2,1)} %reshape.46), calls=%async_computation | async-start | bytes 2359296 | tf_op jit(solution)/shard_map/all_to_all | solution.py:129
  38.5 3.1 gather_fusion
  41.7 5.0 %broadcast_select_fusion = bf16[16,256,576]{1,2,0:T(8,128)(2,1)} fusion(bf16[16,256,576]{1,2,0:T(8,128)(2,1)} %gather_fusion, pred[16]{0:T(512)(128)(4,1)S(1)} %and_reduce_fusion), kind=kLoop, calls=%fused_computation.25 | loop fusion | flops 2359296 | bytes 9437200 | tf_op jit(solution)/shard_map/jit(_take)/select_n | solution.py:132
  46.6 16.1 %all-to-all-done = bf16[64,2,4608]{2,1,0:T(2,128)(2,1)S(1)} async-done(((bf16[64,2,4608]{2,1,0:T(2,128)(2,1)}), bf16[64,2,4608]{2,1,0:T(2,128)(2,1)S(1)}, u32[]{:S(2)}, u32[]{:S(2)}) %all-to-all-start) | async-done | bytes 1179680 | tf_op jit(solution)/shard_map/all_to_all | solution.py:129
  62.7 7.5 %all-to-all-start.1 = ((bf16[16,256,576]{1,2,0:T(8,128)(2,1)}), bf16[16,256,576]{1,2,0:T(8,128)(2,1)}, u32[]{:S(2)}, u32[]{:S(2)}) async-start(bf16[16,256,576]{1,2,0:T(8,128)(2,1)} %broadcast_select_fusion), calls=%async_computation.1 | async-start | bytes 9437184 | tf_op jit(solution)/shard_map/all_to_all | solution.py:136
  74.2 1.3 fusion.54
  76.8 1.8 copy.43
  78.6 3.6 %fusion.60 = (f32[16,4,2,8]{3,2,0,1:T(2,128)S(1)}, f32[16,4,2,8,2]{3,4,2,0,1:T(2,128)S(1)}) fusion(bf16[4,2,576]{2,1,0:T(2,128)(2,1)S(1)} %copy-done.4, bf16[16,4,2,8,576]{4,3,2,1,0:T(8,128)(2,1)S(1)} %reshape.66, pred[2,2]{1,0:T(4,128)(4,1)S(1)} %iota_compare_fusion), kind=kOutput, calls=%fused_computation.72 | convolution fusion | flops 2364416 | bytes 1201156 | tf_op jit(solution)/shard_map/gcshk,ctk->gcsht/dot_general | solution.py:15
  82.6 74.4 %all-to-all-done.1 = bf16[16,256,576]{1,2,0:T(8,128)(2,1)} async-done(((bf16[16,256,576]{1,2,0:T(8,128)(2,1)}), bf16[16,256,576]{1,2,0:T(8,128)(2,1)}, u32[]{:S(2)}, u32[]{:S(2)}) %all-to-all-start.1) | async-done | bytes 4718624 | tf_op jit(solution)/shard_map/all_to_all | solution.py:136
  157.0 5.2 %copy.66 = bf16[16,72,8,256]{3,2,0,1:T(8,128)(2,1)} copy(bf16[16,72,8,256]{3,2,1,0:T(8,128)(2,1)} %bitcast.27) | data formatting | bytes 9437184 | tf_op jit(solution)/shard_map/reshape | solution.py:137
  162.2 14.7 %while.28 = (s32[]{:T(128)}, f32[16,4,2,8]{0,3,2,1:T(8,128)S(1)}, f32[16,4,2,8]{0,3,2,1:T(8,128)S(1)}, pred[4096]{0:T(1024)(128)(4,1)S(1)}, bf16[4096,576]{0,1:T...) while((s32[]{:T(128)}, f32[16,4,2,8]{0,3,2,1:T(8,128)S(1)}, ...), condition=%wide.region_5.6_spmd, body=%wide.region_2.5_spmd.sunk | while | flops 2430601216 | bytes 20377756 | solution.py:51
  162.2 5.4 %bitcast_reduce_fusion.2 = (f32[16,4,2,8]{0,3,2,1:T(8,128)S(1)}, f32[2048,16,4,2,8]{0,1,4,3,2:T(8,128)S(1)}) fusion(pred[2048]{0:T(1024)(128)(4,1)S(1)} %dynamic_slice.61, bf16[16,4,2,8,576]{4,0,3,2,1:T(8,128)(2,1)S(1)} %get-tuple-element.422, bf16[4096,576]{0,1:T(8,128)(2,1)} %get-tuple-element.421, s32[]{:T(128)S(6)} %select_n.132), kind=kOutput, calls=%fused_computation.2.clone.1 | convolution fusion | flops 2422209536 | bytes 11933700 | tf_op jit(solution)/shard_map/while/body/eval_jaxpr/gcshk,lk->gcshl/dot_general | solution.py:32
  167.6 1.9 fusion.72
  169.6 5.4 %bitcast_reduce_fusion.2 = (f32[16,4,2,8]{0,3,2,1:T(8,128)S(1)}, f32[2048,16,4,2,8]{0,1,4,3,2:T(8,128)S(1)}) fusion(pred[2048]{0:T(1024)(128)(4,1)S(1)} %dynamic_slice.61, bf16[16,4,2,8,576]{4,0,3,2,1:T(8,128)(2,1)S(1)} %get-tuple-element.422, bf16[4096,576]{0,1:T(8,128)(2,1)} %get-tuple-element.421, s32[]{:T(128)S(6)} %select_n.132), kind=kOutput, calls=%fused_computation.2.clone.1 | convolution fusion | flops 2422209536 | bytes 11933700 | tf_op jit(solution)/shard_map/while/body/eval_jaxpr/gcshk,lk->gcshl/dot_general | solution.py:32
  175.0 1.9 fusion.72
  178.1 18.1 %while.29 = (s32[]{:T(128)}, f32[16,4,2,8,512]{4,3,2,1,0:T(8,128)S(1)}, pred[4096]{0:T(1024)(128)(4,1)S(1)}, bf16[4096,576]{0,1:T(8,128)(2,1)}, bf16[16,4,2,8,57...) while((s32[]{:T(128)}, ...), condition=%wide.region_7.8_spmd, body=%wide.region_6.7_spmd.sunk | while | flops 4574412800 | bytes 9976991 | solution.py:80
  178.4 9.0 %fusion.76 = f32[16,4,2,8,512]{4,3,2,1,0:T(8,128)S(1)} fusion(f32[16,4,2,8,512]{4,3,2,1,0:T(8,128)S(1)} %get-tuple-element.439, bf16[4096,576]{0,1:T(8,128)(2,1)} %get-tuple-element.452, s32[]{:T(128)S(6)} %select_n.134, f32[16,4,2,8]{3,2,1,0:T(2,128)S(1)} %get-tuple-element.455, f32[16,4,2,8]{3,2,1,0:T(2,128)S(1)} %get-tuple-element.454, ...), kind=kOutput, calls=%fused_computation.18.clone.1 | convolution fusion | flops 4574412800 | bytes 9972736 | tf_op jit(solution)/shard_map/while/body/eval_jaxpr/gcshl,lk->gcshk/dot_general | solution.py:73
  187.4 8.9 %fusion.76 = f32[16,4,2,8,512]{4,3,2,1,0:T(8,128)S(1)} fusion(f32[16,4,2,8,512]{4,3,2,1,0:T(8,128)S(1)} %get-tuple-element.439, bf16[4096,576]{0,1:T(8,128)(2,1)} %get-tuple-element.452, s32[]{:T(128)S(6)} %select_n.134, f32[16,4,2,8]{3,2,1,0:T(2,128)S(1)} %get-tuple-element.455, f32[16,4,2,8]{3,2,1,0:T(2,128)S(1)} %get-tuple-element.454, ...), kind=kOutput, calls=%fused_computation.18.clone.1 | convolution fusion | flops 4574412800 | bytes 9972736 | tf_op jit(solution)/shard_map/while/body/eval_jaxpr/gcshl,lk->gcshk/dot_general | solution.py:73
  197.5 21.7 %all-to-all-start.2 = ((bf16[16,4,2,8,512]{4,3,2,1,0:T(8,128)(2,1)}), bf16[16,4,2,8,512]{4,3,2,1,0:T(8,128)(2,1)S(1)}, u32[]{:S(2)}, u32[]{:S(2)}) async-start(bf16[16,4,2,8,512]{4,3,2,1,0:T(8,128)(2,1)} %convert_element_type.27), calls=%async_computation.2 | async-start | bytes 2097152 | tf_op jit(solution)/shard_map/all_to_all | solution.py:150
  220.5 21.7 %all-to-all-done.2 = bf16[16,4,2,8,512]{4,3,2,1,0:T(8,128)(2,1)S(1)} async-done(((bf16[16,4,2,8,512]{4,3,2,1,0:T(8,128)(2,1)}), bf16[16,4,2,8,512]{4,3,2,1,0:T(8,128)(2,1)S(1)}, u32[]{:S(2)}, u32[]{:S(2)}) %all-to-all-start.2) | async-done | bytes 1048608 | tf_op jit(solution)/shard_map/all_to_all | solution.py:150
  243.5 9.4 %fusion.22 = f32[64,2,7168]{2,0,1:T(8,128)} fusion(bf16[1024,7168]{1,0:T(8,128)(2,1)} %param.21, bf16[8,2,8,8,128]{4,3,2,1,0:T(8,128)(2,1)S(1)} %fusion.26), kind=kOutput, calls=%fused_computation.22 | convolution fusion | flops 1879048192 | bytes 18612224 | tf_op jit(solution)/shard_map/dot_general | solution.py:159
  252.8 87.5 %all-reduce.2 = bf16[64,2,7168]{2,0,1:T(8,128)(2,1)} all-reduce(f32[64,2,7168]{2,0,1:T(8,128)} %fusion.22), channel_id=2, replica_groups=mesh['grp'=2,'xfer'=16] {'xfer'}, use_global_device_ids=true, to_apply=%region_8.9.clone | all-reduce | flops 917504 | bytes 5505024
  (55 shorter events, 12.7 us)
Async XLA Ops:
  0.0 38.5 %copy-start = (bf16[8,256,576]{1,2,0:T(8,128)(2,1)S(1)}, bf16[8,256,576]{1,2,0:T(8,128)(2,1)}, u32[]{:S(2)}) copy-start(bf16[8,256,576]{1,2,0:T(8,128)(2,1)} %param.15) | copy-start | bytes 7077892
  32.6 5.0 %copy-start.5 = (s32[64]{0:T(128)S(1)}, s32[64]{0:T(128)}, u32[]{:S(2)}) copy-start(s32[64]{0:T(128)} %param.18) | copy-start | bytes 772
  33.9 28.8 %all-to-all-start = ((bf16[64,2,4608]{2,1,0:T(2,128)(2,1)}), bf16[64,2,4608]{2,1,0:T(2,128)(2,1)S(1)}, u32[]{:S(2)}, u32[]{:S(2)}) async-start(bf16[64,2,4608]{2,1,0:T(2,128)(2,1)} %reshape.46), calls=%async_computation | async-start | bytes 2359296 | tf_op jit(solution)/shard_map/all_to_all | solution.py:129
  46.6 26.2 %copy-start.7 = (s32[8]{0:T(128)S(1)}, s32[8]{0:T(128)}, u32[]{:S(2)}) copy-start(s32[8]{0:T(128)} %param.17) | copy-start | bytes 100
  46.6 26.9 %copy-start.8 = (s32[8]{0:T(128)S(1)}, s32[8]{0:T(128)}, u32[]{:S(2)}) copy-start(s32[8]{0:T(128)} %param.16) | copy-start | bytes 100
  62.7 94.3 %all-to-all-start.1 = ((bf16[16,256,576]{1,2,0:T(8,128)(2,1)}), bf16[16,256,576]{1,2,0:T(8,128)(2,1)}, u32[]{:S(2)}, u32[]{:S(2)}) async-start(bf16[16,256,576]{1,2,0:T(8,128)(2,1)} %broadcast_select_fusion), calls=%async_computation.1 | async-start | bytes 9437184 | tf_op jit(solution)/shard_map/all_to_all | solution.py:136
  70.2 8.4 %copy-start.4 = (bf16[4,2,576]{2,1,0:T(2,128)(2,1)S(1)}, bf16[4,2,576]{2,1,0:T(2,128)(2,1)}, u32[]{:S(2)}) copy-start(bf16[4,2,576]{2,1,0:T(2,128)(2,1)} %param.14) | copy-start | bytes 27652
  76.8 5.4 %copy-start.2 = (bf16[16,4,2,8,576]{4,3,2,1,0:T(8,128)(2,1)}, bf16[16,4,2,8,576]{4,3,2,1,0:T(8,128)(2,1)S(1)}, u32[]{:S(2)}) copy-start(bf16[16,4,2,8,576]{4,3,2,1,0:T(8,128)(2,1)S(1)} %reshape.66) | copy-start | bytes 3538948
  157.0 5.2 %copy-start.3 = (bf16[16,4,2,8,576]{4,0,3,2,1:T(8,128)(2,1)S(1)}, bf16[16,4,2,8,576]{4,0,3,2,1:T(8,128)(2,1)}, u32[]{:S(2)}) copy-start(bf16[16,4,2,8,576]{4,0,3,2,1:T(8,128)(2,1)} %copy.43) | copy-start | bytes 3538948
  196.3 22.9 %copy-start.9 = (u32[32]{0:T(128)S(1)}, u32[32]{0:T(128)}, u32[]{:S(2)}) copy-start(u32[32]{0:T(128)} %constant.170) | copy-start | bytes 388
  196.3 45.9 %copy-start.6 = (bf16[8,512,128]{2,1,0:T(8,128)(2,1)S(1)}, bf16[8,512,128]{2,1,0:T(8,128)(2,1)}, u32[]{:S(2)}) copy-start(bf16[8,512,128]{2,1,0:T(8,128)(2,1)} %param.20) | copy-start | bytes 3145732
  197.5 44.7 %all-to-all-start.2 = ((bf16[16,4,2,8,512]{4,3,2,1,0:T(8,128)(2,1)}), bf16[16,4,2,8,512]{4,3,2,1,0:T(8,128)(2,1)S(1)}, u32[]{:S(2)}, u32[]{:S(2)}) async-start(bf16[16,4,2,8,512]{4,3,2,1,0:T(8,128)(2,1)} %convert_element_type.27), calls=%async_computation.2 | async-start | bytes 2097152 | tf_op jit(solution)/shard_map/all_to_all | solution.py:150
  243.5 98.6 %copy-start.1 = (bf16[8,256,576]{1,2,0:T(8,128)(2,1)S(1)}, bf16[8,256,576]{1,2,0:T(8,128)(2,1)}, u32[]{:S(2)}) copy-start(bf16[8,256,576]{1,2,0:T(8,128)(2,1)} %param.15) | copy-start | bytes 7077892
where the time goes:
time: 344 us; the launch traced here: 342 us
  blocking collectives  112 us (33%)
  waiting for transfers between devices  112 us (33%)
  matrix products  50.5 us (15%)
  starting transfers between devices  33 us (10%)
  local copies, waits for them, and re-layouts  18.7 us (5%)
  other arithmetic  12.4 us (4%)
    unnamed x1, blocking collectives  87.5 us
    all_to_all x1, waiting for transfers between devices, shards(): lax.all_to_all(outgoing, 'xfer', split_axis=0, concat_axis=0, tiled=True)  74.4 us
    all_gather x1, blocking collectives, shards(): part_rows = lax.all_gather(cq, 'xfer', axis=0, tiled=True)  24.5 us
    all_to_all x1, starting transfers between devices, shards(): lax.all_to_all(compressed_states, 'xfer', split_axis=0, concat_axis=0, ti...  21.7 us
    all_to_all x1, waiting for transfers between devices, shards(): lax.all_to_all(compressed_states, 'xfer', split_axis=0, concat_axis=0, ti...  21.7 us
    dot_general x2, matrix products, accumulate(): jnp.einsum('gcshl,lk->gcshk', weights, block_keys[:, :latent_width], pref...  17.8 us
    all_to_all x1, waiting for transfers between devices, shards(): lax.all_to_all(head_queries, 'xfer', split_axis=0, concat_axis=0, tiled=T...  16.1 us
    dot_general x2, matrix products, block_scores(): jnp.einsum('gcshk,lk->gcshl', queries_here, block_keys, preferred_element...  10.8 us
  transfers between devices with their start and end apart: 3, of which 3 were waited for; matrix products, arithmetic and copies ran while one was open for 6% of the time, Pallas kernels for 0%

commit v1 on v0

v1 whole, which is shorter than its diff:
```python
import functools

import jax
import jax.numpy as jnp
from jax import lax
from jax.experimental import pallas as pl
from jax.experimental.pallas import tpu as pltpu
from jax.sharding import PartitionSpec as P

SCORE_SCALE = 0.135
BF16 = jnp.bfloat16
F32 = jnp.float32
ANY = pl.BlockSpec(memory_space=pl.ANY)
VMEM = pl.BlockSpec(memory_space=pltpu.VMEM)
MIB = 1 << 20


def greet(n, me):
    barrier = pltpu.get_barrier_semaphore()

    def hello(j, carry):
        pl.semaphore_signal(
            barrier, inc=1, device_id={"xfer": lax.rem(me + j, n)},
            device_id_type=pl.DeviceIdType.MESH,
        )
        return carry

    lax.fori_loop(1, n, hello, 0)
    pl.semaphore_wait(barrier, n - 1)


def remote(src, dst, send, recv, device):
    return pltpu.make_async_remote_copy(
        src_ref=src, dst_ref=dst, send_sem=send, recv_sem=recv,
        device_id={"xfer": device}, device_id_type=pl.DeviceIdType.MESH,
    )


def loop(low, high, body):
    def step(i, carry):
        body(i)
        return carry

    lax.fori_loop(low, high, step, 0)


def exchange_kernel(
    n, cq_ref, wq_ref, out_ref, q_ref, k_ref,
    cq_all, wq_v, qs, wq_sem, cq_send, cq_recv, q_send, q_recv,
    k_send, k_recv, f_send, f_recv, local_sem,
):
    me = lax.axis_index("xfer")
    chips = n // 2
    chip = me // 2
    core = lax.rem(me, 2)
    sibling = chip * 2 + 1 - core
    pairs = wq_v.shape[0]
    width = wq_v.shape[2]
    kv = width // 2
    rows = cq_ref.shape[0]

    def load_wq(p):
        return pltpu.make_async_copy(
            wq_ref.at[:, pl.ds(pl.multiple_of(p * width, 128), width)], wq_v.at[p], wq_sem.at[p]
        )

    loop(0, pairs, lambda p: load_wq(p).start())
    own_block = pltpu.make_async_copy(out_ref.at[chip], k_ref.at[me], local_sem.at[0])
    own_block.start()
    greet(n, me)

    def cq_copy(j):
        return remote(
            cq_ref, cq_all.at[me], cq_send.at[j], cq_recv.at[me], lax.rem(me + j, n)
        )

    loop(1, n, lambda j: cq_copy(j).start())
    cq_all[me] = cq_ref[...]

    def block_copy(j, half):
        target = lax.rem(chip + j, chips)
        return remote(
            out_ref.at[target, half], k_ref.at[me, half],
            k_send.at[j, half], k_recv.at[me], target * 2 + half,
        )

    def send_blocks(j):
        block_copy(j, 0).start()
        block_copy(j, 1).start()

    sibling_copy = remote(
        out_ref.at[chip], k_ref.at[me], k_send.at[0, 0], k_recv.at[me], sibling
    )
    sibling_copy.start()
    loop(1, chips, send_blocks)

    def wait_cq(j):
        s = lax.rem(me + n - j, n)
        remote(cq_ref, cq_all.at[s], cq_send.at[j], cq_recv.at[s], s).wait_recv()

    loop(1, n, wait_cq)
    x = cq_all[...].reshape(n * rows, cq_ref.shape[1]).astype(BF16)

    def project(p):
        load_wq(p).wait()
        y = jnp.dot(x, wq_v[p], preferred_element_type=F32)
        first = y[:, :kv].reshape(n, rows, kv)
        second = y[:, kv:].reshape(n, rows, kv)
        qs[:, pl.ds(pl.multiple_of(p * 2 * rows, 16), 2 * rows), :] = jnp.concatenate(
            [first, second], axis=1
        ).astype(BF16)

    loop(0, pairs, project)

    def q_copy(j):
        d = lax.rem(me + j, n)
        return remote(qs.at[d], q_ref.at[me], q_send.at[j], q_recv.at[me], d)

    loop(1, n, lambda j: q_copy(j).start())
    own_q = pltpu.make_async_copy(qs.at[me], q_ref.at[me], local_sem.at[1])
    own_q.start()

    def forward_copy(s):
        return remote(k_ref.at[s, core], k_ref.at[s, core], f_send.at[s], f_recv.at[s], sibling)

    def source(j, other):
        return lax.rem(chip + chips - j, chips) * 2 + other

    def relay(j):
        for other in (0, 1):
            s = source(j, other)
            remote(
                out_ref.at[0, 0], k_ref.at[s, core], k_send.at[0, 0], k_recv.at[s], s
            ).wait_recv()
            forward_copy(s).start()

    loop(1, chips, relay)

    def finish(j):
        for other in (0, 1):
            s = source(j, other)
            remote(
                k_ref.at[s, 1 - core], k_ref.at[s, 1 - core], f_send.at[s], f_recv.at[s], sibling
            ).wait_recv()
            forward_copy(s).wait_send()
        block_copy(j, 0).wait_send()
        block_copy(j, 1).wait_send()

    loop(1, chips, finish)
    sibling_copy.wait_send()
    remote(
        out_ref.at[chip], k_ref.at[sibling], k_send.at[0, 0], k_recv.at[sibling], sibling
    ).wait_recv()

    def finish_q(j):
        s = lax.rem(me + n - j, n)
        remote(qs.at[me], q_ref.at[s], q_send.at[j], q_recv.at[s], s).wait_recv()
        q_copy(j).wait_send()
        cq_copy(j).wait_send()

    loop(1, n, finish_q)
    own_q.wait()
    own_block.wait()


def attend_kernel(
    n, key_chunk, q_ref, k_ref, live_ref, own_key_ref, own_bias_ref, lat_ref,
    lat_out, score, total, l_send, l_recv, local_sem,
):
    me = lax.axis_index("xfer")
    per_source = q_ref.shape[1]
    kv = q_ref.shape[2]
    latent = lat_ref.shape[2]
    block = score.shape[0]
    keys = k_ref.shape[0]
    group = block // per_source
    blocks = n // group
    chunks = keys // key_chunk
    own_width = own_key_ref.shape[0]
    nt = (((1,), (1,)), ((), ()))
    greet(n, me)

    def lat_copy(d):
        return remote(lat_out.at[d], lat_ref.at[me], l_send.at[d], l_recv.at[me], d)

    def own_copy():
        return pltpu.make_async_copy(lat_out.at[me], lat_ref.at[me], local_sem)

    def each_block(b):
        first = lax.rem(me // group + 1 + b, blocks) * group
        q = q_ref[pl.ds(first, group)].reshape(block, kv)
        own = (
            lax.dot_general(q, own_key_ref[...], nt, preferred_element_type=F32) * SCORE_SCALE
            + own_bias_ref[...]
        )

        def scores(c, top):
            at = pl.ds(pl.multiple_of(c * key_chunk, key_chunk), key_chunk)
            s = (
                lax.dot_general(q, k_ref[at, :], nt, preferred_element_type=F32) * SCORE_SCALE
                + live_ref[:, at]
            )
            score[:, at] = s
            for i in range(0, key_chunk, 128):
                top = jnp.maximum(top, s[:, i : i + 128])
            return top

        top = lax.fori_loop(0, chunks, scores, own)
        top = jnp.max(top, axis=1, keepdims=True)
        own = jnp.exp(own - top)

        def sums(c, acc):
            at = pl.ds(pl.multiple_of(c * key_chunk, key_chunk), key_chunk)
            e = jnp.exp(score[:, at] - top)
            score[:, at] = e
            for i in range(0, key_chunk, 128):
                acc = acc + e[:, i : i + 128]
            return acc

        acc = lax.fori_loop(0, chunks, sums, own)
        inverse = 1.0 / jnp.sum(acc, axis=1, keepdims=True)
        total[...] = jnp.dot(
            (own * inverse).astype(BF16), own_key_ref[:, :latent], preferred_element_type=F32
        )

        def gather(c):
            at = pl.ds(pl.multiple_of(c * key_chunk, key_chunk), key_chunk)
            total[...] += jnp.dot(
                (score[:, at] * inverse).astype(BF16), k_ref[at, :latent],
                preferred_element_type=F32,
            )

        loop(0, chunks, gather)
        lat_out[pl.ds(first, group)] = total[...].astype(BF16).reshape(group, per_source, latent)

        def send(i):
            d = first + i

            @pl.when(d != me)
            def _():
                lat_copy(d).start()

            @pl.when(d == me)
            def _():
                own_copy().start()

        loop(0, group, send)

    loop(0, blocks, each_block)

    def finish(j):
        s = lax.rem(me + j, n)
        remote(lat_out.at[me], lat_ref.at[s], l_send.at[s], l_recv.at[s], s).wait_recv()
        lat_copy(s).wait_send()

    loop(1, n, finish)
    own_copy().wait()


def output_kernel(
    n, lat_ref, up_ref, wo_ref, o_ref,
    hv, wo_v, part, x_in, snd, rcv, wo_sem, x_send, x_recv, s_send, s_recv,
):
    me = lax.axis_index("xfer")
    chips = n // 2
    chip = me // 2
    core = lax.rem(me, 2)
    sibling = chip * 2 + 1 - core
    chunks = wo_v.shape[0]
    cw = wo_v.shape[3]
    half = chunks * cw
    heads, latent, value = up_ref.shape
    rows = lat_ref.shape[1] // heads

    def load_wo(j, side):
        return pltpu.make_async_copy(
            wo_ref.at[:, pl.ds(pl.multiple_of(j * cw + side * half, 128), cw)],
            wo_v.at[j, side], wo_sem.at[j, side],
        )

    def load(j):
        load_wo(j, 0).start()
        load_wo(j, 1).start()

    loop(0, chunks, load)
    greet(n, me)
    for p in range(heads // 2):
        z = lat_ref[:, p * 2 * rows : (p + 1) * 2 * rows, :].astype(F32)
        for i in (0, 1):
            h = 2 * p + i
            z_head = z[:, i * rows : (i + 1) * rows, :].reshape(n * rows, latent).astype(BF16)
            y = jnp.dot(z_head, up_ref[h], preferred_element_type=F32)
            y = y.reshape(chips, 2, rows, value)
            hv[0 : chips * rows, h * value : (h + 1) * value] = (
                y[:, 0].reshape(chips * rows, value).astype(BF16)
            )
            hv[chips * rows :, h * value : (h + 1) * value] = (
                y[:, 1].reshape(chips * rows, value).astype(BF16)
            )

    def core_copy(j):
        return remote(part.at[j, 1 - core], x_in.at[j], x_send.at[j], x_recv.at[j], sibling)

    def multiply(j):
        for side in (0, 1):
            load_wo(j, side).wait()
            y = jnp.dot(hv[...], wo_v[j, side], preferred_element_type=F32)
            part[j, 0, side] = y[: chips * rows]
            part[j, 1, side] = y[chips * rows :]
        core_copy(j).start()

    def chip_copy(j, i):
        t = lax.rem(chip + i, chips)
        return remote(
            snd.at[j, t], rcv.at[j, chip], s_send.at[j, i], s_recv.at[j, chip], t * 2 + core
        )

    def combine(j):
        core_copy(j).wait_recv()
        both = part[j, core] + x_in[j]
        packed = jnp.concatenate(
            [both[0].reshape(chips, rows, cw), both[1].reshape(chips, rows, cw)], axis=1
        )
        snd[j] = packed.astype(BF16)
        loop(1, chips, lambda i: chip_copy(j, i).start())

    multiply(0)

    def step(j):
        multiply(j)
        combine(j - 1)

    loop(1, chunks, step)
    combine(chunks - 1)

    def finish(j):
        def wait(i):
            s = lax.rem(chip + chips - i, chips)
            remote(
                snd.at[j, 0], rcv.at[j, s], s_send.at[j, i], s_recv.at[j, s], s * 2 + core
            ).wait_recv()
            chip_copy(j, i).wait_send()

        loop(1, chips, wait)
        core_copy(j).wait_send()
        rcv[j, chip] = snd[j, chip]
        y = jnp.sum(rcv[j].astype(F32), axis=0)
        o_ref[:, pl.ds(pl.multiple_of(j * cw, 128), cw)] = y[:rows].astype(BF16)
        o_ref[:, pl.ds(pl.multiple_of(half + j * cw, 128), cw)] = y[rows:].astype(BF16)

    loop(0, chunks, finish)


def params(collective_id, mib):
    return pltpu.CompilerParams(
        collective_id=collective_id, has_side_effects=True, vmem_limit_bytes=mib * MIB
    )


def shards(cq, new_kv, cache, prompt_len, prefill_owner, cand_req, w_q, value_up_weight, w_o):
    n = lax.axis_size("xfer")
    device = lax.axis_index("xfer")
    cand, steps, q_width = cq.shape
    heads, latent, value = value_up_weight.shape
    segment, kv = cache.shape[1:]
    length = segment * n
    rows = cand * steps
    model = w_o.shape[1]
    per_source = heads * rows
    chips = n // 2
    dma = pltpu.SemaphoreType.DMA

    request_of_chip = cand_req.reshape(chips, 2 * cand)[:, 0]
    outgoing = jnp.take(cache, request_of_chip, axis=0, mode="clip").reshape(
        chips, 2, segment // 2, kv
    )
    my_request = lax.dynamic_index_in_dim(request_of_chip, device // 2, 0, keepdims=False)
    my_length = lax.dynamic_index_in_dim(prompt_len, my_request, 0, keepdims=False)
    first_owner = lax.dynamic_index_in_dim(prefill_owner, my_request, 0, keepdims=False)
    row_index = jnp.arange(length, dtype=jnp.int32)
    position = (row_index // segment - first_owner) % n * segment + row_index % segment
    live = jnp.where(position < my_length, 0.0, -jnp.inf).astype(F32)[None, :]

    pairs = heads // 2
    queries, keys = pl.pallas_call(
        functools.partial(exchange_kernel, n),
        out_shape=(
            jax.ShapeDtypeStruct((n, per_source, kv), BF16),
            jax.ShapeDtypeStruct((n, 2, segment // 2, kv), BF16),
        ),
        in_specs=[VMEM, ANY, ANY],
        out_specs=(ANY, ANY),
        scratch_shapes=[
            pltpu.VMEM((n, rows, q_width), F32),
            pltpu.VMEM((pairs, q_width, 2 * kv), BF16),
            pltpu.VMEM((n, per_source, kv), BF16),
            dma((pairs,)),
            dma((n,)), dma((n,)), dma((n,)), dma((n,)),
            dma((chips, 2)), dma((n,)), dma((n,)), dma((n,)),
            dma((2,)),
        ],
        compiler_params=params(0, 40),
        name="exchange",
    )(cq.reshape(rows, q_width).astype(F32), w_q, outgoing)

    block = 256
    own_keys = jnp.zeros((128, kv), BF16).at[:rows].set(new_kv.reshape(rows, kv))
    row = jnp.arange(block, dtype=jnp.int32)[:, None] % rows
    col = jnp.arange(128, dtype=jnp.int32)[None, :]
    seen = (col // steps == row // steps) & (col % steps <= row % steps)
    own_bias = jnp.where(seen, 0.0, -jnp.inf).astype(F32)
    latents = pl.pallas_call(
        functools.partial(attend_kernel, n, 512),
        out_shape=jax.ShapeDtypeStruct((n, per_source, latent), BF16),
        in_specs=[VMEM] * 5,
        out_specs=ANY,
        scratch_shapes=[
            pltpu.VMEM((n, per_source, latent), BF16),
            pltpu.VMEM((block, length), F32),
            pltpu.VMEM((block, latent), F32),
            dma((n,)), dma((n,)), dma,
        ],
        compiler_params=params(1, 48),
        name="attend",
    )(queries, keys.reshape(length, kv), live, own_keys, own_bias)

    cw = 512
    chunks = model // (2 * cw)
    out = pl.pallas_call(
        functools.partial(output_kernel, n),
        out_shape=jax.ShapeDtypeStruct((rows, model), BF16),
        in_specs=[VMEM, VMEM, ANY],
        out_specs=VMEM,
        scratch_shapes=[
            pltpu.VMEM((n * rows, heads * value), BF16),
            pltpu.VMEM((chunks, 2, heads * value, cw), BF16),
            pltpu.VMEM((chunks, 2, 2, chips * rows, cw), F32),
            pltpu.VMEM((chunks, 2, chips * rows, cw), F32),
            pltpu.VMEM((chunks, chips, 2 * rows, cw), BF16),
            pltpu.VMEM((chunks, chips, 2 * rows, cw), BF16),
            dma((chunks, 2)), dma((chunks,)), dma((chunks,)),
            dma((chunks, chips)), dma((chunks, chips)),
        ],
        compiler_params=params(2, 44),
        name="output",
    )(latents, value_up_weight, w_o)
    return out.reshape(cand, steps, model)


def solution(mesh):
    in_specs = (
        P(("grp", "xfer"), None, None),
        P(("grp", "xfer"), None, None),
        P("grp", "xfer", None),
        P("grp"),
        P("grp"),
        P("grp"),
        P(None, "xfer"),
        P("xfer", None, None),
        P("xfer", None),
    )
    out_specs = P(("grp", "xfer"), None, None)
    return jax.shard_map(shards, mesh=mesh, in_specs=in_specs, out_specs=out_specs, check_vma=False)
```

time: 344 us -> 200 us (0.58)
  Pallas kernels: 0 us -> 178 us
  blocking collectives: 112 us -> 0 us
  waiting for transfers between devices: 112 us -> 0 us
  matrix products: 50.5 us -> 0 us
  starting transfers between devices: 33 us -> 0 us
  other arithmetic: 12.4 us -> 1.58 us
    pallas_call x0 -> x3, Pallas kernels: none -> 178 us  [the longest x1 98.2 us: shards(): pl.pallas_call(functools.partial(exchange_kernel, n), out_shape=(jax.Shap...]
    all_to_all x3 -> x0, waiting for transfers between devices: 112 us -> none  [the longest x1 74.4 us: shards(): lax.all_to_all(outgoing, 'xfer', split_axis=0, concat_axis=0, tiled=True)]
    unnamed x1 -> x0, blocking collectives: 87.5 us -> none
    dot_general x9 -> x0, matrix products: 50.5 us -> none  [the longest x2 17.8 us: accumulate(): jnp.einsum('gcshl,lk->gcshk', weights, block_keys[:, :latent_width], pref...]
    all_to_all x3 -> x0, starting transfers between devices: 33 us -> none  [the longest x1 21.7 us: shards(): lax.all_to_all(compressed_states, 'xfer', split_axis=0, concat_axis=0, ti...]
    all_gather x1 -> x0, blocking collectives: 24.5 us -> none  [shards(): part_rows = lax.all_gather(cq, 'xfer', axis=0, tiled=True)]
    reshape x5 -> x2, local copies, waits for them, and re-layouts: 8.7 us -> 1.42 us  [the longest x1 0.73 us: shards(): request_of_chip = cand_req.reshape(chips, 2 * cand)[:, 0]]
    unnamed x21 -> x18, local copies, waits for them, and re-layouts: 0.64 us -> 6.46 us
  transfers between devices with their start and end apart: 3 -> 0, of which waited for: 3 -> 0; matrix products, arithmetic and copies ran while one was open for 6% -> 0% of each run, Pallas kernels for 0% -> 0%
where the time goes in v1:
time: 200 us; the launch traced here: 199 us
  Pallas kernels  178 us (89%)
  local copies, waits for them, and re-layouts  17.2 us (9%)
  between operations  2.07 us (1%)
    pallas_call x1, Pallas kernels, shards(): pl.pallas_call(functools.partial(exchange_kernel, n), out_shape=(jax.Shap...  98.2 us
    pallas_call x1, Pallas kernels, shards(): pl.pallas_call(functools.partial(attend_kernel, n, 512), out_shape=jax.Sh...  52.1 us
    pallas_call x1, Pallas kernels, shards(): pl.pallas_call(functools.partial(output_kernel, n), out_shape=jax.ShapeDt...  28.1 us
    gather x2, local copies, waits for them, and re-layouts, shards(): jnp.take(cache, request_of_chip, axis=0, mode='clip')  6.48 us
    unnamed x18, local copies, waits for them, and re-layouts  6.46 us

profile of v1, /device:TPU:0, one launch (start us, length us, event | category | flops | bytes accessed | tf_op | source)
XLA Modules:
  0.0 199.2 jit_solution(8398661785565655663)
XLA Ops:
  0.0 0.0 copy-start
  0.0 0.9 reshape.266.cq_ref
  0.9 0.7 reshape.261
  1.6 0.1 fusion.4
  1.8 0.0 copy-done
  1.8 2.1 %gather_fusion = bf16[8,256,576]{1,2,0:T(8,128)(2,1)} fusion(bf16[8,256,576]{1,2,0:T(8,128)(2,1)S(1)} %copy-done, s32[1024]{0:T(1024)S(1)} %pad_clamp_fusion), kind=kCustom, calls=%fused_computation | custom fusion | bytes 4718624 | tf_op jit(solution)/shard_map/jit(_take)/gather | solution.py:374
  3.9 4.3 %copy.11 = bf16[8,256,576]{2,1,0:T(8,128)(2,1)} copy(bf16[8,256,576]{1,2,0:T(8,128)(2,1)} %gather_fusion) | data formatting | bytes 4718592 | tf_op jit(solution)/shard_map/jit(_take)/gather | solution.py:374
  8.3 1.7 copy-done.1
  10.0 98.2 %exchange.1 = (bf16[16,64,576]{2,1,0:T(8,128)(2,1)S(1)}, bf16[16,2,128,576]{3,2,1,0:T(8,128)(2,1)S(1)}) custom-call(f32[8,1536]{1,0:T(8,128)S(1)} %reshape.266.cq_ref, bf16[1536,4608]{1,0:T(8,128)(2,1)} %wq_ref.1, bf16[8,2,128,576]{3,2,1,0:T(8,128)(2,1)S(1)} %bitcast.5), custom_call_target="tpu_custom_call" | custom-call | tf_op jit(solution)/shard_map/exchange/pallas_call | solution.py:385
  108.2 0.0 copy-start.2
  108.2 2.3 %copy-done.2 = bf16[16,2,128,576]{3,2,1,0:T(8,128)(2,1)} copy-done((bf16[16,2,128,576]{3,2,1,0:T(8,128)(2,1)}, bf16[16,2,128,576]{3,2,1,0:T(8,128)(2,1)S(1)}, u32[]{:S(2)}) %copy-start.2) | copy-done | bytes 4718616
  110.5 1.1 copy-done.3
  111.6 0.5 constant_dynamic-slice_fusion
  114.1 0.0 copy-done.7
  114.1 0.6 dynamic_slice.12
  114.7 0.0 copy-done.8
  114.7 0.7 dynamic_slice.11
  115.3 1.4 compare_select_fusion.2.live_ref
  116.7 0.0 copy-done.6
  116.8 0.1 and_select_fusion.own_bias_ref
  117.0 1.3 copy-done.4
  118.3 52.1 %attend.1.lat_ref = bf16[16,64,512]{2,1,0:T(8,128)(2,1)S(1)} custom-call(bf16[16,64,576]{2,1,0:T(8,128)(2,1)S(1)} %copy-done.4, bf16[4096,576]{1,0:T(8,128)(2,1)} %bitcast.6, f32[1,4096]{1,0:T(1,128)S(1)} %compare_select_fusion.2.live_ref, bf16[128,576]{1,0:T(8,128)(2,1)S(1)} %scatter.4.own_key_ref, f32[256,128]{1,0:T(8,128)S(1)} %and_select_fusion.own_bias_ref), custom_call_target="tpu_custom_call" | custom-call | tf_op jit(solution)/shard_map/attend/pallas_call | solution.py:412
  170.4 28.1 %output.1 = bf16[8,7168]{1,0:T(8,128)(2,1)S(1)} custom-call(bf16[16,64,512]{2,1,0:T(8,128)(2,1)S(1)} %attend.1.lat_ref, bf16[8,512,128]{2,1,0:T(8,128)(2,1)S(1)} %copy-done.5, bf16[1024,7168]{1,0:T(8,128)(2,1)} %wo_ref.1), custom_call_target="tpu_custom_call" | custom-call | tf_op jit(solution)/shard_map/output/pallas_call | solution.py:429
  198.5 0.7 reshape.265
  (13 shorter events, 0.1 us)
Async XLA Ops:
  0.0 1.8 copy-start
  8.2 1.7 copy-start.1
  10.0 104.1 %copy-start.7 = (s32[8]{0:T(128)S(1)}, s32[8]{0:T(128)}, u32[]{:S(2)}) copy-start(s32[8]{0:T(128)} %param.14) | copy-start | bytes 100
  10.0 104.7 %copy-start.8 = (s32[8]{0:T(128)S(1)}, s32[8]{0:T(128)}, u32[]{:S(2)}) copy-start(s32[8]{0:T(128)} %param.15) | copy-start | bytes 100
  10.0 106.8 %copy-start.6 = (bf16[4,2,576]{2,1,0:T(2,128)(2,1)S(1)}, bf16[4,2,576]{2,1,0:T(2,128)(2,1)}, u32[]{:S(2)}) copy-start(bf16[4,2,576]{2,1,0:T(2,128)(2,1)} %param.12) | copy-start | bytes 27652
  108.2 2.3 %copy-start.2 = (bf16[16,2,128,576]{3,2,1,0:T(8,128)(2,1)}, bf16[16,2,128,576]{3,2,1,0:T(8,128)(2,1)S(1)}, u32[]{:S(2)}) copy-start(bf16[16,2,128,576]{3,2,1,0:T(8,128)(2,1)S(1)} %get-tuple-element.20) | copy-start | bytes 14155780
  110.5 1.1 copy-start.3
  117.0 1.3 copy-start.4
  118.3 52.1 %copy-start.5 = (bf16[8,512,128]{2,1,0:T(8,128)(2,1)S(1)}, bf16[8,512,128]{2,1,0:T(8,128)(2,1)}, u32[]{:S(2)}) copy-start(bf16[8,512,128]{2,1,0:T(8,128)(2,1)} %up_ref.1) | copy-start | bytes 3145732

commit v2 on v1

v2 whole, which is shorter than its diff:
```python
import functools

import jax
import jax.numpy as jnp
from jax import lax
from jax.experimental import pallas as pl
from jax.experimental.pallas import tpu as pltpu
from jax.sharding import PartitionSpec as P

SCORE_SCALE = 0.135
BF16 = jnp.bfloat16
F32 = jnp.float32
ANY = pl.BlockSpec(memory_space=pl.ANY)
VMEM = pl.BlockSpec(memory_space=pltpu.VMEM)
MIB = 1 << 20


def greet(n, me):
    barrier = pltpu.get_barrier_semaphore()

    def hello(j, carry):
        pl.semaphore_signal(
            barrier, inc=1, device_id={"xfer": me ^ j},
            device_id_type=pl.DeviceIdType.MESH,
        )
        return carry

    lax.fori_loop(1, n, hello, 0)
    pl.semaphore_wait(barrier, n - 1)


def remote(src, dst, send, recv, device):
    return pltpu.make_async_remote_copy(
        src_ref=src, dst_ref=dst, send_sem=send, recv_sem=recv,
        device_id={"xfer": device}, device_id_type=pl.DeviceIdType.MESH,
    )


def loop(low, high, body):
    def step(i, carry):
        body(i)
        return carry

    lax.fori_loop(low, high, step, 0)


def prepare_kernel(cand, request_ref, length_ref, owner_ref, cache_ref, own_ref,
                   out_ref, live_ref, own_key_ref, sems):
    chips, _, width = live_ref.shape
    segment = width // 2

    def pick(t):
        return pltpu.make_async_copy(
            cache_ref.at[request_ref[t * 2 * cand]], out_ref.at[t], sems.at[t]
        )

    loop(0, chips, lambda t: pick(t).start())
    request = request_ref[lax.axis_index("xfer") // 2 * 2 * cand]
    chip = lax.broadcasted_iota(jnp.int32, live_ref.shape, 0)
    col = lax.broadcasted_iota(jnp.int32, live_ref.shape, 2)
    odd = (col >= segment).astype(jnp.int32)
    order = chip * 2 + odd - owner_ref[request]
    order = jnp.where(order < 0, order + 2 * chips, order)
    position = order * segment + col - odd * segment
    live_ref[...] = jnp.where(position < length_ref[request], 0.0, -jnp.inf).astype(F32)
    own_key_ref[...] = jnp.zeros_like(own_key_ref)
    own_key_ref[: own_ref.shape[0]] = own_ref[...]
    loop(0, chips, lambda t: pick(t).wait())


def attend_kernel(
    n, steps, early, cq_ref, wq_ref, out_ref, live_ref, own_key_ref, lat_ref,
    cq_all, wq_v, qs, q_in, k_in, lat_out, score, own_score, top_ref, sum_ref, total,
    wq_sem, cq_send, cq_recv, q_send, q_recv, k_send, k_recv, f_send, f_recv,
    l_send, l_recv, local_sem,
):
    me = lax.axis_index("xfer")
    chips = n // 2
    chip = me // 2
    core = lax.rem(me, 2)
    sibling = me ^ 1
    pairs, _, width = wq_v.shape
    kv = width // 2
    rows = cq_ref.shape[0]
    per_source, latent = lat_out.shape[1:]
    pair_keys = live_ref.shape[2]
    block = total.shape[0]
    group = block // per_source
    blocks = n // group
    nt = (((1,), (1,)), ((), ()))

    def load_wq(p):
        return pltpu.make_async_copy(
            wq_ref.at[:, pl.ds(pl.multiple_of(p * width, 128), width)], wq_v.at[p], wq_sem.at[p]
        )

    loop(0, pairs, lambda p: load_wq(p).start())
    own_block = pltpu.make_async_copy(out_ref.at[chip], k_in.at[me], local_sem.at[0])
    own_block.start()
    greet(n, me)

    def cq_copy(j):
        return remote(cq_ref, cq_all.at[me], cq_send.at[j], cq_recv.at[me], me ^ j)

    loop(1, n, lambda j: cq_copy(j).start())
    cq_all[me] = cq_ref[...]

    def block_copy(j, half):
        t = chip ^ j
        return remote(
            out_ref.at[t, half], k_in.at[me, half], k_send.at[j, half], k_recv.at[me], t * 2 + half
        )

    def send_blocks(r):
        block_copy(chips - r, 0).start()
        block_copy(chips - r, 1).start()

    sibling_copy = remote(
        out_ref.at[chip], k_in.at[me], k_send.at[0, 0], k_recv.at[me], sibling
    )
    loop(1, early, send_blocks)

    def wait_cq(j):
        s = me ^ j
        remote(cq_ref, cq_all.at[s], cq_send.at[j], cq_recv.at[s], s).wait_recv()

    loop(1, n, wait_cq)
    x = cq_all[...].reshape(n * rows, cq_ref.shape[1]).astype(BF16)

    def project(p):
        load_wq(p).wait()
        y = jnp.dot(x, wq_v[p], preferred_element_type=F32)
        first = y[:, :kv].reshape(n, rows, kv)
        second = y[:, kv:].reshape(n, rows, kv)
        qs[:, pl.ds(pl.multiple_of(p * 2 * rows, 16), 2 * rows), :] = jnp.concatenate(
            [first, second], axis=1
        ).astype(BF16)

    loop(0, pairs, project)

    def q_copy(j):
        return remote(qs.at[me ^ j], q_in.at[me], q_send.at[j], q_recv.at[me], me ^ j)

    loop(1, n, lambda r: q_copy(n - r).start())
    sibling_copy.start()
    loop(early, chips, send_blocks)
    q_in[me] = qs[me]

    row = lax.rem(lax.broadcasted_iota(jnp.int32, (block, 128), 0), rows)
    col = lax.broadcasted_iota(jnp.int32, (block, 128), 1)
    behind = row - col
    seen = (behind >= 0) & (behind <= lax.rem(row, steps))
    own_bias = jnp.where(seen, 0.0, -jnp.inf).astype(F32)

    def wait_q(r):
        s = me ^ (n - r)
        remote(qs.at[me], q_in.at[s], q_send.at[n - r], q_recv.at[s], s).wait_recv()

    loop(1, n, wait_q)

    def queries(b):
        return q_in[pl.ds(b * group, group)].reshape(block, kv)

    def own_terms(b):
        s = (
            lax.dot_general(queries(b), own_key_ref[...], nt, preferred_element_type=F32)
            * SCORE_SCALE
            + own_bias
        )
        own_score[b] = s
        top = jnp.maximum(s, -1e30)
        top_ref[b] = top
        sum_ref[b] = jnp.exp(s - top)

    loop(0, blocks, own_terms)

    def pair_scores(t):
        keys = k_in[pl.ds(2 * t, 2)].reshape(pair_keys, kv)
        live = live_ref[t]

        def block_scores(b):
            s = (
                lax.dot_general(queries(b), keys, nt, preferred_element_type=F32) * SCORE_SCALE
                + live
            )
            score[b, t] = s
            old = top_ref[b]
            top = old
            for i in range(0, pair_keys, 128):
                top = jnp.maximum(top, s[:, i : i + 128])
            acc = sum_ref[b] * jnp.exp(old - top)
            for i in range(0, pair_keys, 128):
                acc = acc + jnp.exp(s[:, i : i + 128] - top)
            top_ref[b] = top
            sum_ref[b] = acc

        loop(0, blocks, block_scores)

    def forward_copy(s):
        return remote(k_in.at[s, core], k_in.at[s, core], f_send.at[s], f_recv.at[s], sibling)

    def relay(t):
        for other in (0, 1):
            s = t * 2 + other
            remote(
                out_ref.at[0, 0], k_in.at[s, core], k_send.at[0, 0], k_recv.at[s], s
            ).wait_recv()
            forward_copy(s).start()

    def arrive(t):
        for other in (0, 1):
            s = t * 2 + other
            remote(
                k_in.at[s, 1 - core], k_in.at[s, 1 - core], f_send.at[s], f_recv.at[s], sibling
            ).wait_recv()

    relay(chip ^ (chips - 1))

    def receive(r):
        relay(chip ^ (chips - r))
        t = chip ^ (chips - r + 1)
        arrive(t)
        pair_scores(t)

    loop(2, chips, receive)
    own_block.wait()
    remote(
        out_ref.at[chip], k_in.at[sibling], k_send.at[0, 0], k_recv.at[sibling], sibling
    ).wait_recv()
    pair_scores(chip)
    arrive(chip ^ 1)
    pair_scores(chip ^ 1)

    def lat_copy(d):
        return remote(lat_out.at[d], lat_ref.at[me], l_send.at[d], l_recv.at[me], d)

    def own_copy():
        return pltpu.make_async_copy(lat_out.at[me], lat_ref.at[me], local_sem.at[1])

    def each_block(r):
        b = (me // group) ^ (blocks - 1 - r)
        lane_top = top_ref[b]
        top = jnp.max(lane_top, axis=1, keepdims=True)
        inverse = 1.0 / jnp.sum(sum_ref[b] * jnp.exp(lane_top - top), axis=1, keepdims=True)
        total[...] = jnp.dot(
            (jnp.exp(own_score[b] - top) * inverse).astype(BF16), own_key_ref[:, :latent],
            preferred_element_type=F32,
        )

        def gather(t):
            weights = (jnp.exp(score[b, t] - top) * inverse).astype(BF16)
            values = k_in[pl.ds(2 * t, 2)].reshape(pair_keys, kv)[:, :latent]
            total[...] += jnp.dot(weights, values, preferred_element_type=F32)

        loop(0, chips, gather)
        first = b * group
        lat_out[pl.ds(first, group)] = total[...].astype(BF16).reshape(group, per_source, latent)

        def send(i):
            d = first + i

            @pl.when(d != me)
            def _():
                lat_copy(d).start()

            @pl.when(d == me)
            def _():
                own_copy().start()

        loop(0, group, send)

    loop(0, blocks, each_block)

    def finish(j):
        s = me ^ j
        q_copy(j).wait_send()
        cq_copy(j).wait_send()
        remote(lat_out.at[me], lat_ref.at[s], l_send.at[s], l_recv.at[s], s).wait_recv()
        lat_copy(s).wait_send()

    def finish_blocks(j):
        for half in (0, 1):
            block_copy(j, half).wait_send()
            forward_copy((chip ^ j) * 2 + half).wait_send()

    sibling_copy.wait_send()
    loop(1, chips, finish_blocks)
    loop(1, n, finish)
    own_copy().wait()


def output_kernel(
    n, lat_ref, up_ref, wo_ref, o_ref,
    hv, wo_v, part, x_in, snd, rcv, wo_sem, x_send, x_recv, s_send, s_recv,
):
    me = lax.axis_index("xfer")
    chips = n // 2
    chip = me // 2
    core = lax.rem(me, 2)
    sibling = chip * 2 + 1 - core
    chunks = wo_v.shape[0]
    cw = wo_v.shape[3]
    half = chunks * cw
    heads, latent, value = up_ref.shape
    rows = lat_ref.shape[1] // heads

    def load_wo(j, side):
        return pltpu.make_async_copy(
            wo_ref.at[:, pl.ds(pl.multiple_of(j * cw + side * half, 128), cw)],
            wo_v.at[j, side], wo_sem.at[j, side],
        )

    def load(j):
        load_wo(j, 0).start()
        load_wo(j, 1).start()

    loop(0, chunks, load)
    greet(n, me)
    for p in range(heads // 2):
        z = lat_ref[:, p * 2 * rows : (p + 1) * 2 * rows, :].astype(F32)
        for i in (0, 1):
            h = 2 * p + i
            z_head = z[:, i * rows : (i + 1) * rows, :].reshape(n * rows, latent).astype(BF16)
            y = jnp.dot(z_head, up_ref[h], preferred_element_type=F32)
            y = y.reshape(chips, 2, rows, value)
            hv[0 : chips * rows, h * value : (h + 1) * value] = (
                y[:, 0].reshape(chips * rows, value).astype(BF16)
            )
            hv[chips * rows :, h * value : (h + 1) * value] = (
                y[:, 1].reshape(chips * rows, value).astype(BF16)
            )

    def core_copy(j):
        return remote(part.at[j, 1 - core], x_in.at[j], x_send.at[j], x_recv.at[j], sibling)

    def multiply(j):
        for side in (0, 1):
            load_wo(j, side).wait()
            y = jnp.dot(hv[...], wo_v[j, side], preferred_element_type=F32)
            part[j, 0, side] = y[: chips * rows]
            part[j, 1, side] = y[chips * rows :]
        core_copy(j).start()

    def chip_copy(j, i):
        t = chip ^ i
        return remote(
            snd.at[j, t], rcv.at[j, chip], s_send.at[j, i], s_recv.at[j, chip], t * 2 + core
        )

    def combine(j):
        core_copy(j).wait_recv()
        both = part[j, core] + x_in[j]
        packed = jnp.concatenate(
            [both[0].reshape(chips, rows, cw), both[1].reshape(chips, rows, cw)], axis=1
        )
        snd[j] = packed.astype(BF16)
        loop(1, chips, lambda i: chip_copy(j, chips - i).start())

    multiply(0)

    def step(j):
        multiply(j)
        combine(j - 1)

    loop(1, chunks, step)
    combine(chunks - 1)

    def finish(j):
        def wait(i):
            s = chip ^ i
            remote(
                snd.at[j, 0], rcv.at[j, s], s_send.at[j, i], s_recv.at[j, s], s * 2 + core
            ).wait_recv()
            chip_copy(j, i).wait_send()

        loop(1, chips, wait)
        core_copy(j).wait_send()
        rcv[j, chip] = snd[j, chip]
        y = jnp.sum(rcv[j].astype(F32), axis=0)
        o_ref[:, pl.ds(pl.multiple_of(j * cw, 128), cw)] = y[:rows].astype(BF16)
        o_ref[:, pl.ds(pl.multiple_of(half + j * cw, 128), cw)] = y[rows:].astype(BF16)

    loop(0, chunks, finish)


def params(collective_id, mib):
    return pltpu.CompilerParams(
        collective_id=collective_id, has_side_effects=True, vmem_limit_bytes=mib * MIB
    )


def shards(cq, new_kv, cache, prompt_len, prefill_owner, cand_req, w_q, value_up_weight, w_o):
    n = lax.axis_size("xfer")
    cand, steps, q_width = cq.shape
    heads, latent, value = value_up_weight.shape
    segment, kv = cache.shape[1:]
    rows = cand * steps
    model = w_o.shape[1]
    per_source = heads * rows
    chips = n // 2
    dma = pltpu.SemaphoreType.DMA

    smem = pl.BlockSpec(memory_space=pltpu.SMEM)
    outgoing, live, own_keys = pl.pallas_call(
        functools.partial(prepare_kernel, cand),
        out_shape=(
            jax.ShapeDtypeStruct((chips, segment, kv), BF16),
            jax.ShapeDtypeStruct((chips, 1, 2 * segment), F32),
            jax.ShapeDtypeStruct((128, kv), BF16),
        ),
        in_specs=[smem, smem, smem, ANY, VMEM],
        out_specs=(ANY, VMEM, VMEM),
        scratch_shapes=[dma((chips,))],
        name="prepare",
    )(cand_req, prompt_len, prefill_owner, cache, new_kv.reshape(rows, kv))

    pairs = heads // 2
    block = 256
    blocks = n * per_source // block
    latents = pl.pallas_call(
        functools.partial(attend_kernel, n, steps, chips // 4 + 1),
        out_shape=jax.ShapeDtypeStruct((n, per_source, latent), BF16),
        in_specs=[VMEM, ANY, ANY, VMEM, VMEM],
        out_specs=ANY,
        scratch_shapes=[
            pltpu.VMEM((n, rows, q_width), F32),
            pltpu.VMEM((pairs, q_width, 2 * kv), BF16),
            pltpu.VMEM((n, per_source, kv), BF16),
            pltpu.VMEM((n, per_source, kv), BF16),
            pltpu.VMEM((n, 2, segment // 2, kv), BF16),
            pltpu.VMEM((n, per_source, latent), BF16),
            pltpu.VMEM((blocks, chips, block, 2 * segment), F32),
            pltpu.VMEM((blocks, block, 128), F32),
            pltpu.VMEM((blocks, block, 128), F32),
            pltpu.VMEM((blocks, block, 128), F32),
            pltpu.VMEM((block, latent), F32),
            dma((pairs,)),
            dma((n,)), dma((n,)), dma((n,)), dma((n,)),
            dma((chips, 2)), dma((n,)), dma((n,)), dma((n,)),
            dma((n,)), dma((n,)), dma((2,)),
        ],
        compiler_params=params(0, 60),
        name="attend",
    )(
        cq.reshape(rows, q_width).astype(F32), w_q,
        outgoing.reshape(chips, 2, segment // 2, kv), live, own_keys,
    )

    cw = 512
    chunks = model // (2 * cw)
    out = pl.pallas_call(
        functools.partial(output_kernel, n),
        out_shape=jax.ShapeDtypeStruct((rows, model), BF16),
        in_specs=[VMEM, VMEM, ANY],
        out_specs=VMEM,
        scratch_shapes=[
            pltpu.VMEM((n * rows, heads * value), BF16),
            pltpu.VMEM((chunks, 2, heads * value, cw), BF16),
            pltpu.VMEM((chunks, 2, 2, chips * rows, cw), F32),
            pltpu.VMEM((chunks, 2, chips * rows, cw), F32),
            pltpu.VMEM((chunks, chips, 2 * rows, cw), BF16),
            pltpu.VMEM((chunks, chips, 2 * rows, cw), BF16),
            dma((chunks, 2)), dma((chunks,)), dma((chunks,)),
            dma((chunks, chips)), dma((chunks, chips)),
        ],
        compiler_params=params(1, 44),
        name="output",
    )(latents, value_up_weight, w_o)
    return out.reshape(cand, steps, model)


def solution(mesh):
    in_specs = (
        P(("grp", "xfer"), None, None),
        P(("grp", "xfer"), None, None),
        P("grp", "xfer", None),
        P("grp"),
        P("grp"),
        P("grp"),
        P(None, "xfer"),
        P("xfer", None, None),
        P("xfer", None),
    )
    out_specs = P(("grp", "xfer"), None, None)
    return jax.shard_map(shards, mesh=mesh, in_specs=in_specs, out_specs=out_specs, check_vma=False)
```

time: 200 us -> 266 us (1.33)
  Pallas kernels: 178 us -> 258 us
  local copies, waits for them, and re-layouts: 17.2 us -> 7.55 us
    pallas_call x2, Pallas kernels: 150 us -> 229 us  [the longest x1 147 us: shards(): pl.pallas_call(functools.partial(attend_kernel, n, steps, chips // 4 + 1)...]
    gather x2 -> x0, local copies, waits for them, and re-layouts: 6.48 us -> none  [shards(): jnp.take(cache, request_of_chip, axis=0, mode='clip')]
    unnamed x18 -> x9, local copies, waits for them, and re-layouts: 6.46 us -> 5.61 us
where the time goes in v2:
time: 266 us
  Pallas kernels  258 us (97%)
  local copies, waits for them, and re-layouts  7.55 us (3%)
    pallas_call x1, Pallas kernels, shards(): pl.pallas_call(functools.partial(attend_kernel, n, steps, chips // 4 + 1)...  147 us
    pallas_call x1, Pallas kernels, shards(): pl.pallas_call(functools.partial(prepare_kernel, cand), out_shape=(jax.Sh...  82 us
    pallas_call x1, Pallas kernels, shards(): pl.pallas_call(functools.partial(output_kernel, n), out_shape=jax.ShapeDt...  29.2 us
    unnamed x9, local copies, waits for them, and re-layouts  5.61 us

profile of v2, /device:TPU:0, one launch (start us, length us, event | category | flops | bytes accessed | tf_op | source)
XLA Modules:
  0.0 266.0 jit_solution(11458099393781453152)
XLA Ops:
  0.0 0.0 copy-start.3
  0.0 0.0 copy-start.2
  0.0 4.4 %copy.10.cache_ref = bf16[8,256,576]{2,1,0:T(8,128)(2,1)} copy(bf16[8,256,576]{1,2,0:T(8,128)(2,1)} %param.11) | data formatting | bytes 4718592 | tf_op args[2]
  4.4 0.0 copy-done.3
  4.4 0.6 reshape.12.own_ref
  5.0 82.0 %prepare.1 = (bf16[8,256,576]{2,1,0:T(8,128)(2,1)}, f32[8,1,512]{2,1,0:T(1,128)}, bf16[128,576]{1,0:T(8,128)(2,1)}) custom-call(s32[64]{0:T(128)} %request_ref.1, s32[8]{0:T(128)} %length_ref.1, s32[8]{0:T(128)} %owner_ref.1, bf16[8,256,576]{2,1,0:T(8,128)(2,1)} %copy.10.cache_ref, bf16[8,576]{1,0:T(8,128)(2,1)} %reshape.12.own_ref), custom_call_target="tpu_custom_call" | custom-call | tf_op jit(solution)/shard_map/prepare/pallas_call | solution.py:404
  87.0 0.0 copy-done.2
  87.0 0.6 reshape.15.cq_ref
  87.6 0.0 copy-start.1
  87.6 147.2 %attend.1.lat_ref = bf16[16,64,512]{2,1,0:T(8,128)(2,1)} custom-call(f32[8,1536]{1,0:T(8,128)} %reshape.15.cq_ref, bf16[1536,4608]{1,0:T(8,128)(2,1)} %wq_ref.1, bf16[8,2,128,576]{3,2,1,0:T(8,128)(2,1)} %bitcast.1, f32[8,1,512]{2,1,0:T(1,128)} %get-tuple-element.9.live_ref, bf16[128,576]{1,0:T(8,128)(2,1)} %get-tuple-element.10.own_key_ref), custom_call_target="tpu_custom_call" | custom-call | tf_op jit(solution)/shard_map/attend/pallas_call | solution.py:420
  234.8 0.0 copy-done.1
  234.8 0.0 copy-start
  234.8 1.2 copy-done
  236.1 29.2 %output.1 = bf16[8,7168]{1,0:T(8,128)(2,1)S(1)} custom-call(bf16[16,64,512]{2,1,0:T(8,128)(2,1)S(1)} %copy-done, bf16[8,512,128]{2,1,0:T(8,128)(2,1)S(1)} %copy-done.1, bf16[1024,7168]{1,0:T(8,128)(2,1)} %wo_ref.1), custom_call_target="tpu_custom_call" | custom-call | tf_op jit(solution)/shard_map/output/pallas_call | solution.py:451
  265.3 0.7 reshape.14
Async XLA Ops:
  0.0 4.4 %copy-start.3 = (bf16[4,2,576]{2,1,0:T(2,128)(2,1)S(1)}, bf16[4,2,576]{2,1,0:T(2,128)(2,1)}, u32[]{:S(2)}) copy-start(bf16[4,2,576]{2,1,0:T(2,128)(2,1)} %param.10) | copy-start | bytes 27652
  0.0 87.0 %copy-start.2 = (bf16[4,2,1536]{2,1,0:T(2,128)(2,1)S(1)}, bf16[4,2,1536]{2,1,0:T(2,128)(2,1)}, u32[]{:S(2)}) copy-start(bf16[4,2,1536]{2,1,0:T(2,128)(2,1)} %param.9) | copy-start | bytes 73732
  87.6 147.2 %copy-start.1 = (bf16[8,512,128]{2,1,0:T(8,128)(2,1)S(1)}, bf16[8,512,128]{2,1,0:T(8,128)(2,1)}, u32[]{:S(2)}) copy-start(bf16[8,512,128]{2,1,0:T(8,128)(2,1)} %up_ref.1) | copy-start | bytes 3145732
  234.8 1.2 copy-start

commit v3 on v2

--- a/solution.py
+++ b/solution.py
@@ -44,66 +44,36 @@
     lax.fori_loop(low, high, step, 0)
 
 
-def prepare_kernel(cand, request_ref, length_ref, owner_ref, cache_ref, own_ref,
-                   out_ref, live_ref, own_key_ref, sems):
-    chips, _, width = live_ref.shape
-    segment = width // 2
-
-    def pick(t):
-        return pltpu.make_async_copy(
-            cache_ref.at[request_ref[t * 2 * cand]], out_ref.at[t], sems.at[t]
-        )
-
-    loop(0, chips, lambda t: pick(t).start())
-    request = request_ref[lax.axis_index("xfer") // 2 * 2 * cand]
-    chip = lax.broadcasted_iota(jnp.int32, live_ref.shape, 0)
-    col = lax.broadcasted_iota(jnp.int32, live_ref.shape, 2)
-    odd = (col >= segment).astype(jnp.int32)
-    order = chip * 2 + odd - owner_ref[request]
-    order = jnp.where(order < 0, order + 2 * chips, order)
-    position = order * segment + col - odd * segment
-    live_ref[...] = jnp.where(position < length_ref[request], 0.0, -jnp.inf).astype(F32)
-    own_key_ref[...] = jnp.zeros_like(own_key_ref)
-    own_key_ref[: own_ref.shape[0]] = own_ref[...]
-    loop(0, chips, lambda t: pick(t).wait())
-
-
 def attend_kernel(
-    n, steps, early, cq_ref, wq_ref, out_ref, live_ref, own_key_ref, lat_ref,
-    cq_all, wq_v, qs, q_in, k_in, lat_out, score, own_score, top_ref, sum_ref, total,
+    n, cand, steps, early, request_ref, length_ref, owner_ref, cq_ref, wq_ref, cache_ref,
+    own_key_ref, lat_ref,
+    cq_all, qs, q_in, out_ref, k_in, v_in, lat_out, own_score, top_ref, sum_ref, total,
     wq_sem, cq_send, cq_recv, q_send, q_recv, k_send, k_recv, f_send, f_recv,
-    l_send, l_recv, local_sem,
+    l_send, l_recv, c_send, c_recv, local_sem,
 ):
     me = lax.axis_index("xfer")
     chips = n // 2
     chip = me // 2
     core = lax.rem(me, 2)
     sibling = me ^ 1
-    pairs, _, width = wq_v.shape
-    kv = width // 2
-    rows = cq_ref.shape[0]
+    kv = q_in.shape[2]
+    width = 2 * kv
+    pairs = wq_ref.shape[1] // width
+    rows = cq_ref.shape[0] // 2
     per_source, latent = lat_out.shape[1:]
-    pair_keys = live_ref.shape[2]
+    half_keys = k_in.shape[3]
+    segment = 2 * half_keys
+    pair_keys = 2 * segment
     block = total.shape[0]
     group = block // per_source
     blocks = n // group
     nt = (((1,), (1,)), ((), ()))
 
-    def load_wq(p):
-        return pltpu.make_async_copy(
-            wq_ref.at[:, pl.ds(pl.multiple_of(p * width, 128), width)], wq_v.at[p], wq_sem.at[p]
-        )
-
-    loop(0, pairs, lambda p: load_wq(p).start())
-    own_block = pltpu.make_async_copy(out_ref.at[chip], k_in.at[me], local_sem.at[0])
-    own_block.start()
-    greet(n, me)
-
     def cq_copy(j):
-        return remote(cq_ref, cq_all.at[me], cq_send.at[j], cq_recv.at[me], me ^ j)
-
-    loop(1, n, lambda j: cq_copy(j).start())
-    cq_all[me] = cq_ref[...]
+        return remote(cq_ref, cq_all.at[me], cq_send.at[j], cq_recv.at[me], me ^ (2 * j))
+
+    def cq_forward(s):
+        return remote(cq_all.at[s], cq_all.at[s], c_send.at[s], c_recv.at[s], sibling)
 
     def block_copy(j, half):
         t = chip ^ j
@@ -118,25 +88,71 @@
     sibling_copy = remote(
         out_ref.at[chip], k_in.at[me], k_send.at[0, 0], k_recv.at[me], sibling
     )
-    loop(1, early, send_blocks)
-
-    def wait_cq(j):
-        s = me ^ j
-        remote(cq_ref, cq_all.at[s], cq_send.at[j], cq_recv.at[s], s).wait_recv()
-
-    loop(1, n, wait_cq)
-    x = cq_all[...].reshape(n * rows, cq_ref.shape[1]).astype(BF16)
-
-    def project(p):
-        load_wq(p).wait()
-        y = jnp.dot(x, wq_v[p], preferred_element_type=F32)
-        first = y[:, :kv].reshape(n, rows, kv)
-        second = y[:, kv:].reshape(n, rows, kv)
-        qs[:, pl.ds(pl.multiple_of(p * 2 * rows, 16), 2 * rows), :] = jnp.concatenate(
-            [first, second], axis=1
+
+    def start_phase(wq_v, cache_v):
+        def load_wq(p):
+            return pltpu.make_async_copy(
+                wq_ref.at[:, pl.ds(pl.multiple_of(p * width, 128), width)],
+                wq_v.at[p], wq_sem.at[p],
+            )
+
+        load_cache = pltpu.make_async_copy(cache_ref, cache_v, local_sem.at[0])
+        load_cache.start()
+        loop(0, pairs, lambda p: load_wq(p).start())
+        greet(n, me)
+        loop(1, chips, lambda r: cq_copy(chips - r).start())
+        cq_all[me] = cq_ref[...]
+        cq_forward(me).start()
+        load_cache.wait()
+
+        def stage(r):
+            t = chip ^ (chips - r)
+            block = cache_v[request_ref[t * 2 * cand]]
+            out_ref[t, 0] = block[:, :half_keys]
+            out_ref[t, 1] = block[:, half_keys:]
+
+        def stage_send(r):
+            stage(r)
+            send_blocks(r)
+
+        loop(1, early, stage_send)
+        loop(early, chips + 1, stage)
+        k_in[me] = out_ref[chip]
+
+        def relay_cq(r):
+            s = me ^ (2 * (chips - r))
+            remote(cq_ref, cq_all.at[s], cq_send.at[0], cq_recv.at[s], s).wait_recv()
+            cq_forward(s).start()
+
+        def wait_cq(r):
+            s = me ^ (2 * (chips - r)) ^ 1
+            remote(cq_all.at[s], cq_all.at[s], c_send.at[s], c_recv.at[s], sibling).wait_recv()
+
+        loop(1, chips, relay_cq)
+        loop(1, chips + 1, wait_cq)
+        gathered = cq_all[...].astype(F32)
+        x = jnp.concatenate(
+            [gathered[:, :rows].reshape(n * rows, -1), gathered[:, rows:].reshape(n * rows, -1)],
+            axis=1,
         ).astype(BF16)
 
-    loop(0, pairs, project)
+        def project(p):
+            load_wq(p).wait()
+            y = jnp.dot(x, wq_v[p], preferred_element_type=F32)
+            first = y[:, :kv].reshape(n, rows, kv)
+            second = y[:, kv:].reshape(n, rows, kv)
+            qs[:, pl.ds(pl.multiple_of(p * 2 * rows, 16), 2 * rows), :] = jnp.concatenate(
+                [first, second], axis=1
+            ).astype(BF16)
+
+        loop(0, pairs, project)
+
+    with jax.named_scope("start"):
+        pl.run_scoped(
+            start_phase,
+            pltpu.VMEM((pairs, wq_ref.shape[0], width), BF16),
+            pltpu.VMEM(cache_ref.shape, BF16),
+        )
 
     def q_copy(j):
         return remote(qs.at[me ^ j], q_in.at[me], q_send.at[j], q_recv.at[me], me ^ j)
@@ -156,7 +172,8 @@
         s = me ^ (n - r)
         remote(qs.at[me], q_in.at[s], q_send.at[n - r], q_recv.at[s], s).wait_recv()
 
-    loop(1, n, wait_q)
+    with jax.named_scope("wait_queries"):
+        loop(1, n, wait_q)
 
     def queries(b):
         return q_in[pl.ds(b * group, group)].reshape(block, kv)
@@ -174,13 +191,28 @@
 
     loop(0, blocks, own_terms)
 
-    def pair_scores(t):
-        keys = k_in[pl.ds(2 * t, 2)].reshape(pair_keys, kv)
-        live = live_ref[t]
+    request = request_ref[chip * 2 * cand]
+    prompt = length_ref[request]
+    owner = owner_ref[request]
+
+    def pair_keys_of(t, features):
+        return jnp.concatenate(
+            [k_in[2 * t + i, h, :features, :] for i in (0, 1) for h in (0, 1)], axis=1
+        )
+
+    def pair_scores(score, t):
+        keys = pair_keys_of(t, kv)
+        at = lax.broadcasted_iota(jnp.int32, (1, pair_keys), 1)
+        odd = (at >= segment).astype(jnp.int32)
+        order = t * 2 + odd - owner
+        order = jnp.where(order < 0, order + n, order)
+        live = jnp.where(order * segment + at - odd * segment < prompt, 0.0, -jnp.inf).astype(F32)
+        if v_in is not None:
+            v_in[t] = keys[:latent].T
 
         def block_scores(b):
             s = (
-                lax.dot_general(queries(b), keys, nt, preferred_element_type=F32) * SCORE_SCALE
+                jnp.dot(queries(b), keys, preferred_element_type=F32) * SCORE_SCALE
                 + live
             )
             score[b, t] = s
@@ -214,30 +246,13 @@
                 k_in.at[s, 1 - core], k_in.at[s, 1 - core], f_send.at[s], f_recv.at[s], sibling
             ).wait_recv()
 
-    relay(chip ^ (chips - 1))
-
-    def receive(r):
-        relay(chip ^ (chips - r))
-        t = chip ^ (chips - r + 1)
-        arrive(t)
-        pair_scores(t)
-
-    loop(2, chips, receive)
-    own_block.wait()
-    remote(
-        out_ref.at[chip], k_in.at[sibling], k_send.at[0, 0], k_recv.at[sibling], sibling
-    ).wait_recv()
-    pair_scores(chip)
-    arrive(chip ^ 1)
-    pair_scores(chip ^ 1)
-
     def lat_copy(d):
         return remote(lat_out.at[d], lat_ref.at[me], l_send.at[d], l_recv.at[me], d)
 
     def own_copy():
         return pltpu.make_async_copy(lat_out.at[me], lat_ref.at[me], local_sem.at[1])
 
-    def each_block(r):
+    def each_block(score, r):
         b = (me // group) ^ (blocks - 1 - r)
         lane_top = top_ref[b]
         top = jnp.max(lane_top, axis=1, keepdims=True)
@@ -249,8 +264,12 @@
 
         def gather(t):
             weights = (jnp.exp(score[b, t] - top) * inverse).astype(BF16)
-            values = k_in[pl.ds(2 * t, 2)].reshape(pair_keys, kv)[:, :latent]
-            total[...] += jnp.dot(weights, values, preferred_element_type=F32)
+            if v_in is not None:
+                total[...] += jnp.dot(weights, v_in[t], preferred_element_type=F32)
+            else:
+                total[...] += lax.dot_general(
+                    weights, pair_keys_of(t, latent), nt, preferred_element_type=F32
+                )
 
         loop(0, chips, gather)
         first = b * group
@@ -269,35 +288,68 @@
 
         loop(0, group, send)
 
-    loop(0, blocks, each_block)
+    def main_phase(score):
+        with jax.named_scope("own_scores"):
+            loop(0, blocks, own_terms)
+        relay(chip ^ (chips - 1))
+
+        def receive(r):
+            relay(chip ^ (chips - r))
+            t = chip ^ (chips - r + 1)
+            arrive(t)
+            pair_scores(score, t)
+
+        with jax.named_scope("receive"):
+            loop(2, chips, receive)
+            remote(
+                out_ref.at[chip], k_in.at[sibling], k_send.at[0, 0], k_recv.at[sibling], sibling
+            ).wait_recv()
+            pair_scores(score, chip)
+            arrive(chip ^ 1)
+            pair_scores(score, chip ^ 1)
+        with jax.named_scope("weighted_sums"):
+            loop(0, blocks, lambda r: each_block(score, r))
+
+    pl.run_scoped(main_phase, pltpu.VMEM((blocks, chips, block, pair_keys), F32))
 
     def finish(j):
         s = me ^ j
         q_copy(j).wait_send()
-        cq_copy(j).wait_send()
         remote(lat_out.at[me], lat_ref.at[s], l_send.at[s], l_recv.at[s], s).wait_recv()
         lat_copy(s).wait_send()
 
     def finish_blocks(j):
+        cq_copy(j).wait_send()
         for half in (0, 1):
             block_copy(j, half).wait_send()
             forward_copy((chip ^ j) * 2 + half).wait_send()
 
-    sibling_copy.wait_send()
-    loop(1, chips, finish_blocks)
-    loop(1, n, finish)
-    own_copy().wait()
+    with jax.named_scope("wait_latents"):
+        sibling_copy.wait_send()
+        loop(1, chips, finish_blocks)
+        loop(1, n, finish)
+        loop(0, chips, lambda t: cq_forward(t * 2 + core).wait_send())
+        own_copy().wait()
+
+
+def lean_kernel(*args):
+    at = 4 + 8 + 5
+    attend_kernel(*args[:at], None, *args[at:])
 
 
 def output_kernel(
     n, lat_ref, up_ref, wo_ref, o_ref,
-    hv, wo_v, part, x_in, snd, rcv, wo_sem, x_send, x_recv, s_send, s_recv,
+    hv, wo_v, part, x_in, kept, y_out, y_in, snd, rcv,
+    wo_sem, x_send, x_recv, y_send, y_recv, s_send, s_recv,
 ):
     me = lax.axis_index("xfer")
     chips = n // 2
     chip = me // 2
     core = lax.rem(me, 2)
-    sibling = chip * 2 + 1 - core
+    sibling = me ^ 1
+    lines = chips // 2
+    line = chip // 2
+    side_of_pair = lax.rem(chip, 2)
     chunks = wo_v.shape[0]
     cw = wo_v.shape[3]
     half = chunks * cw
@@ -341,42 +393,57 @@
             part[j, 1, side] = y[chips * rows :]
         core_copy(j).start()
 
-    def chip_copy(j, i):
-        t = chip ^ i
-        return remote(
-            snd.at[j, t], rcv.at[j, chip], s_send.at[j, i], s_recv.at[j, chip], t * 2 + core
-        )
+    def pair_copy(j):
+        return remote(y_out.at[j], y_in.at[j], y_send.at[j], y_recv.at[j], me ^ 2)
 
     def combine(j):
         core_copy(j).wait_recv()
         both = part[j, core] + x_in[j]
         packed = jnp.concatenate(
             [both[0].reshape(chips, rows, cw), both[1].reshape(chips, rows, cw)], axis=1
-        )
-        snd[j] = packed.astype(BF16)
-        loop(1, chips, lambda i: chip_copy(j, chips - i).start())
+        ).reshape(lines, 2, 2 * rows, cw)
+        kept[j] = jnp.where(side_of_pair == 0, packed[:, 0], packed[:, 1])
+        y_out[j] = jnp.where(side_of_pair == 0, packed[:, 1], packed[:, 0]).astype(BF16)
+        pair_copy(j).start()
+
+    def line_copy(j, i):
+        t = line ^ i
+        return remote(
+            snd.at[j, t], rcv.at[j, line], s_send.at[j, i], s_recv.at[j, line], me ^ (4 * i)
+        )
+
+    def spread(j):
+        pair_copy(j).wait_recv()
+        both = kept[j] + y_in[j].astype(F32)
+        kept[j] = both
+        snd[j] = both.astype(BF16)
+        loop(1, lines, lambda i: line_copy(j, lines - i).start())
 
     multiply(0)
+    multiply(1)
+    combine(0)
 
     def step(j):
         multiply(j)
         combine(j - 1)
-
-    loop(1, chunks, step)
+        spread(j - 2)
+
+    loop(2, chunks, step)
     combine(chunks - 1)
+    spread(chunks - 2)
+    spread(chunks - 1)
 
     def finish(j):
-        def wait(i):
-            s = chip ^ i
+        y = kept[j, line]
+        for i in range(1, lines):
+            s = line ^ i
             remote(
-                snd.at[j, 0], rcv.at[j, s], s_send.at[j, i], s_recv.at[j, s], s * 2 + core
+                snd.at[j, 0], rcv.at[j, s], s_send.at[j, i], s_recv.at[j, s], me ^ (4 * i)
             ).wait_recv()
-            chip_copy(j, i).wait_send()
-
-        loop(1, chips, wait)
+            line_copy(j, i).wait_send()
+            y = y + rcv[j, s].astype(F32)
         core_copy(j).wait_send()
-        rcv[j, chip] = snd[j, chip]
-        y = jnp.sum(rcv[j].astype(F32), axis=0)
+        pair_copy(j).wait_send()
         o_ref[:, pl.ds(pl.multiple_of(j * cw, 128), cw)] = y[:rows].astype(BF16)
         o_ref[:, pl.ds(pl.multiple_of(half + j * cw, 128), cw)] = y[rows:].astype(BF16)
 
@@ -401,35 +468,26 @@
     dma = pltpu.SemaphoreType.DMA
 
     smem = pl.BlockSpec(memory_space=pltpu.SMEM)
-    outgoing, live, own_keys = pl.pallas_call(
-        functools.partial(prepare_kernel, cand),
-        out_shape=(
-            jax.ShapeDtypeStruct((chips, segment, kv), BF16),
-            jax.ShapeDtypeStruct((chips, 1, 2 * segment), F32),
-            jax.ShapeDtypeStruct((128, kv), BF16),
-        ),
-        in_specs=[smem, smem, smem, ANY, VMEM],
-        out_specs=(ANY, VMEM, VMEM),
-        scratch_shapes=[dma((chips,))],
-        name="prepare",
-    )(cand_req, prompt_len, prefill_owner, cache, new_kv.reshape(rows, kv))
-
+    cq_rows = cq.reshape(rows, q_width)
+    cq_halves = jnp.concatenate([cq_rows[:, : q_width // 2], cq_rows[:, q_width // 2 :]], axis=0)
+    own_keys = jnp.pad(new_kv.reshape(rows, kv), ((0, 128 - rows), (0, 0)))
     pairs = heads // 2
+    keep = n <= 16
     block = 256
     blocks = n * per_source // block
     latents = pl.pallas_call(
-        functools.partial(attend_kernel, n, steps, chips // 4 + 1),
+        functools.partial(attend_kernel if keep else lean_kernel, n, cand, steps, chips // 4 + 1),
         out_shape=jax.ShapeDtypeStruct((n, per_source, latent), BF16),
-        in_specs=[VMEM, ANY, ANY, VMEM, VMEM],
+        in_specs=[smem, smem, smem, VMEM, ANY, ANY, VMEM],
         out_specs=ANY,
         scratch_shapes=[
-            pltpu.VMEM((n, rows, q_width), F32),
-            pltpu.VMEM((pairs, q_width, 2 * kv), BF16),
+            pltpu.VMEM((n, 2 * rows, q_width // 2), BF16),
             pltpu.VMEM((n, per_source, kv), BF16),
             pltpu.VMEM((n, per_source, kv), BF16),
-            pltpu.VMEM((n, 2, segment // 2, kv), BF16),
+            pltpu.VMEM((chips, 2, kv, segment // 2), BF16),
+            pltpu.VMEM((n, 2, kv, segment // 2), BF16),
+            *([pltpu.VMEM((chips, 2 * segment, latent), BF16)] if keep else []),
             pltpu.VMEM((n, per_source, latent), BF16),
-            pltpu.VMEM((blocks, chips, block, 2 * segment), F32),
             pltpu.VMEM((blocks, block, 128), F32),
             pltpu.VMEM((blocks, block, 128), F32),
             pltpu.VMEM((blocks, block, 128), F32),
@@ -437,13 +495,13 @@
             dma((pairs,)),
             dma((n,)), dma((n,)), dma((n,)), dma((n,)),
             dma((chips, 2)), dma((n,)), dma((n,)), dma((n,)),
-            dma((n,)), dma((n,)), dma((2,)),
+            dma((n,)), dma((n,)), dma((n,)), dma((n,)), dma((2,)),
         ],
         compiler_params=params(0, 60),
         name="attend",
     )(
-        cq.reshape(rows, q_width).astype(F32), w_q,
-        outgoing.reshape(chips, 2, segment // 2, kv), live, own_keys,
+        cand_req, prompt_len, prefill_owner, cq_halves, w_q,
+        jnp.swapaxes(cache, 1, 2), own_keys,
     )
 
     cw = 512
@@ -458,10 +516,10 @@
             pltpu.VMEM((chunks, 2, heads * value, cw), BF16),
             pltpu.VMEM((chunks, 2, 2, chips * rows, cw), F32),
             pltpu.VMEM((chunks, 2, chips * rows, cw), F32),
-            pltpu.VMEM((chunks, chips, 2 * rows, cw), BF16),
-            pltpu.VMEM((chunks, chips, 2 * rows, cw), BF16),
-            dma((chunks, 2)), dma((chunks,)), dma((chunks,)),
-            dma((chunks, chips)), dma((chunks, chips)),
+            pltpu.VMEM((chunks, chips // 2, 2 * rows, cw), F32),
+            *([pltpu.VMEM((chunks, chips // 2, 2 * rows, cw), BF16)] * 4),
+            dma((chunks, 2)), dma((chunks,)), dma((chunks,)), dma((chunks,)), dma((chunks,)),
+            dma((chunks, chips // 2)), dma((chunks, chips // 2)),
         ],
         compiler_params=params(1, 44),
         name="output",

time: 266 us -> 157 us (0.59)
  Pallas kernels: 258 us -> 152 us
  local copies, waits for them, and re-layouts: 7.55 us -> 4.17 us
    pallas_call x2 -> x1, Pallas kernels: 229 us -> 125 us  [shards(): pl.pallas_call(functools.partial(attend_kernel if keep else lean_kernel,...]
    unnamed x9 -> x4, local copies, waits for them, and re-layouts: 5.61 us -> 1.22 us
    pallas_call x1, Pallas kernels: 29.2 us -> 26.5 us  [shards(): pl.pallas_call(functools.partial(output_kernel, n), out_shape=jax.ShapeDt...]
where the time goes in v3:
time: 157 us; the launch traced here: 156 us
  Pallas kernels  152 us (97%)
  local copies, waits for them, and re-layouts  4.17 us (3%)
    pallas_call x1, Pallas kernels, shards(): pl.pallas_call(functools.partial(attend_kernel if keep else lean_kernel,...  125 us
    pallas_call x1, Pallas kernels, shards(): pl.pallas_call(functools.partial(output_kernel, n), out_shape=jax.ShapeDt...  26.5 us

profile of v3, /device:TPU:0, one launch (start us, length us, event | category | flops | bytes accessed | tf_op | source)
XLA Modules:
  0.0 156.5 jit_solution(9839852148432183521)
XLA Ops:
  0.0 0.0 copy-start.1
  0.0 0.8 reshape.10
  0.8 0.8 reshape.9
  1.6 0.6 pad_maximum_fusion.cq_ref
  2.2 0.7 pad.4.own_key_ref
  2.9 125.2 %attend.1.lat_ref = bf16[16,64,512]{2,1,0:T(8,128)(2,1)} custom-call(s32[64]{0:T(128)} %request_ref.1, s32[8]{0:T(128)} %length_ref.1, s32[8]{0:T(128)} %owner_ref.1, bf16[16,768]{1,0:T(8,128)(2,1)} %pad_maximum_fusion.cq_ref, bf16[1536,4608]{1,0:T(8,128)(2,1)} %wq_ref.1, bf16[8,576,256]{2,1,0:T(8,128)(2,1)} %bitcast.1, bf16[128,576]{1,0:T(8,128)(2,1)} %pad.4.own_key_ref), custom_call_target="tpu_custom_call" | custom-call | tf_op jit(solution)/shard_map/attend/pallas_call | solution.py:478
  128.1 0.0 copy-done.1
  128.1 0.0 copy-start
  128.1 1.2 copy-done
  129.3 26.5 %output.1 = bf16[8,7168]{1,0:T(8,128)(2,1)S(1)} custom-call(bf16[16,64,512]{2,1,0:T(8,128)(2,1)S(1)} %copy-done, bf16[8,512,128]{2,1,0:T(8,128)(2,1)S(1)} %copy-done.1, bf16[1024,7168]{1,0:T(8,128)(2,1)} %wo_ref.1), custom_call_target="tpu_custom_call" | custom-call | tf_op jit(solution)/shard_map/output/pallas_call | solution.py:509
  155.8 0.7 reshape.11
  (1 shorter events, 0.0 us)
Async XLA Ops:
  0.0 128.1 %copy-start.1 = (bf16[8,512,128]{2,1,0:T(8,128)(2,1)S(1)}, bf16[8,512,128]{2,1,0:T(8,128)(2,1)}, u32[]{:S(2)}) copy-start(bf16[8,512,128]{2,1,0:T(8,128)(2,1)} %up_ref.1) | copy-start | bytes 3145732
  128.1 1.2 copy-start

commit v4 on v3

--- a/solution.py
+++ b/solution.py
@@ -42,6 +42,11 @@
         return carry
 
     lax.fori_loop(low, high, step, 0)
+
+
+def hop(r, chips):
+    odd = lax.rem(r, 2)
+    return odd * (chips - 1) + (1 - odd) * (chips // 2) - lax.div(r, 2)
 
 
 def attend_kernel(
@@ -82,8 +87,8 @@
         )
 
     def send_blocks(r):
-        block_copy(chips - r, 0).start()
-        block_copy(chips - r, 1).start()
+        block_copy(hop(r, chips), 0).start()
+        block_copy(hop(r, chips), 1).start()
 
     sibling_copy = remote(
         out_ref.at[chip], k_in.at[me], k_send.at[0, 0], k_recv.at[me], sibling
@@ -106,7 +111,7 @@
         load_cache.wait()
 
         def stage(r):
-            t = chip ^ (chips - r)
+            t = chip ^ hop(r, chips)
             block = cache_v[request_ref[t * 2 * cand]]
             out_ref[t, 0] = block[:, :half_keys]
             out_ref[t, 1] = block[:, half_keys:]
@@ -294,19 +299,19 @@
         relay(chip ^ (chips - 1))
 
         def receive(r):
-            relay(chip ^ (chips - r))
-            t = chip ^ (chips - r + 1)
+            relay(chip ^ hop(r, chips))
+            t = chip ^ hop(r - 1, chips)
             arrive(t)
             pair_scores(score, t)
 
         with jax.named_scope("receive"):
-            loop(2, chips, receive)
             remote(
                 out_ref.at[chip], k_in.at[sibling], k_send.at[0, 0], k_recv.at[sibling], sibling
             ).wait_recv()
             pair_scores(score, chip)
-            arrive(chip ^ 1)
-            pair_scores(score, chip ^ 1)
+            loop(2, chips, receive)
+            arrive(chip ^ (chips // 2))
+            pair_scores(score, chip ^ (chips // 2))
         with jax.named_scope("weighted_sums"):
             loop(0, blocks, lambda r: each_block(score, r))
 
@@ -419,19 +424,22 @@
         snd[j] = both.astype(BF16)
         loop(1, lines, lambda i: line_copy(j, lines - i).start())
 
-    multiply(0)
-    multiply(1)
+    for j in range(4):
+        multiply(j)
     combine(0)
+    combine(1)
 
     def step(j):
         multiply(j)
-        combine(j - 1)
-        spread(j - 2)
-
-    loop(2, chunks, step)
+        combine(j - 2)
+        spread(j - 4)
+
+    loop(4, chunks, step)
+    combine(chunks - 2)
+    spread(chunks - 4)
     combine(chunks - 1)
-    spread(chunks - 2)
-    spread(chunks - 1)
+    for j in range(chunks - 3, chunks):
+        spread(j)
 
     def finish(j):
         y = kept[j, line]
@@ -476,7 +484,7 @@
     block = 256
     blocks = n * per_source // block
     latents = pl.pallas_call(
-        functools.partial(attend_kernel if keep else lean_kernel, n, cand, steps, chips // 4 + 1),
+        functools.partial(attend_kernel if keep else lean_kernel, n, cand, steps, chips // 2 + 1),
         out_shape=jax.ShapeDtypeStruct((n, per_source, latent), BF16),
         in_specs=[smem, smem, smem, VMEM, ANY, ANY, VMEM],
         out_specs=ANY,

time: 157 us -> 152 us (0.968)
  Pallas kernels: 152 us -> 147 us
    pallas_call x1, Pallas kernels: 26.5 us -> 22.9 us  [shards(): pl.pallas_call(functools.partial(output_kernel, n), out_shape=jax.ShapeDt...]
where the time goes in v4:
time: 152 us; the launch traced here: 151 us
  Pallas kernels  147 us (97%)
  local copies, waits for them, and re-layouts  4.17 us (3%)
    pallas_call x1, Pallas kernels, shards(): pl.pallas_call(functools.partial(attend_kernel if keep else lean_kernel,...  124 us
    pallas_call x1, Pallas kernels, shards(): pl.pallas_call(functools.partial(output_kernel, n), out_shape=jax.ShapeDt...  22.9 us

profile of v4, /device:TPU:0, one launch (start us, length us, event | category | flops | bytes accessed | tf_op | source)
XLA Modules:
  0.0 151.5 jit_solution(14099053185323971249)
XLA Ops:
  0.0 0.0 copy-start.1
  0.0 0.8 reshape.10
  0.8 0.8 reshape.9
  1.6 0.6 pad_maximum_fusion.cq_ref
  2.2 0.7 pad.4.own_key_ref
  2.9 123.8 %attend.1.lat_ref = bf16[16,64,512]{2,1,0:T(8,128)(2,1)} custom-call(s32[64]{0:T(128)} %request_ref.1, s32[8]{0:T(128)} %length_ref.1, s32[8]{0:T(128)} %owner_ref.1, bf16[16,768]{1,0:T(8,128)(2,1)} %pad_maximum_fusion.cq_ref, bf16[1536,4608]{1,0:T(8,128)(2,1)} %wq_ref.1, bf16[8,576,256]{2,1,0:T(8,128)(2,1)} %bitcast.1, bf16[128,576]{1,0:T(8,128)(2,1)} %pad.4.own_key_ref), custom_call_target="tpu_custom_call" | custom-call | tf_op jit(solution)/shard_map/attend/pallas_call | solution.py:486
  126.7 0.0 copy-done.1
  126.7 0.0 copy-start
  126.7 1.2 copy-done
  127.9 22.9 %output.1 = bf16[8,7168]{1,0:T(8,128)(2,1)S(1)} custom-call(bf16[16,64,512]{2,1,0:T(8,128)(2,1)S(1)} %copy-done, bf16[8,512,128]{2,1,0:T(8,128)(2,1)S(1)} %copy-done.1, bf16[1024,7168]{1,0:T(8,128)(2,1)} %wo_ref.1), custom_call_target="tpu_custom_call" | custom-call | tf_op jit(solution)/shard_map/output/pallas_call | solution.py:517
  150.8 0.7 reshape.11
  (1 shorter events, 0.0 us)
Async XLA Ops:
  0.0 126.7 %copy-start.1 = (bf16[8,512,128]{2,1,0:T(8,128)(2,1)S(1)}, bf16[8,512,128]{2,1,0:T(8,128)(2,1)}, u32[]{:S(2)}) copy-start(bf16[8,512,128]{2,1,0:T(8,128)(2,1)} %up_ref.1) | copy-start | bytes 3145732
  126.7 1.2 copy-start

commit v5 on v4

--- a/solution.py
+++ b/solution.py
@@ -481,7 +481,7 @@
     own_keys = jnp.pad(new_kv.reshape(rows, kv), ((0, 128 - rows), (0, 0)))
     pairs = heads // 2
     keep = n <= 16
-    block = 256
+    block = 512
     blocks = n * per_source // block
     latents = pl.pallas_call(
         functools.partial(attend_kernel if keep else lean_kernel, n, cand, steps, chips // 2 + 1),

time: 152 us -> 151 us (level)
  no operation moved by 1% of the time
where the time goes in v5:
time: 151 us
  Pallas kernels  146 us (97%)
  local copies, waits for them, and re-layouts  4.17 us (3%)
    pallas_call x1, Pallas kernels, shards(): pl.pallas_call(functools.partial(attend_kernel if keep else lean_kernel,...  123 us
    pallas_call x1, Pallas kernels, shards(): pl.pallas_call(functools.partial(output_kernel, n), out_shape=jax.ShapeDt...  23 us

profile of v5, /device:TPU:0, one launch (start us, length us, event | category | flops | bytes accessed | tf_op | source)
XLA Modules:
  0.0 150.7 jit_solution(15074418736933488316)
XLA Ops:
  0.0 0.0 copy-start.1
  0.0 0.8 reshape.10
  0.8 0.8 reshape.9
  1.6 0.6 pad_maximum_fusion.cq_ref
  2.2 0.7 pad.4.own_key_ref
  2.9 122.9 %attend.1.lat_ref = bf16[16,64,512]{2,1,0:T(8,128)(2,1)} custom-call(s32[64]{0:T(128)} %request_ref.1, s32[8]{0:T(128)} %length_ref.1, s32[8]{0:T(128)} %owner_ref.1, bf16[16,768]{1,0:T(8,128)(2,1)} %pad_maximum_fusion.cq_ref, bf16[1536,4608]{1,0:T(8,128)(2,1)} %wq_ref.1, bf16[8,576,256]{2,1,0:T(8,128)(2,1)} %bitcast.1, bf16[128,576]{1,0:T(8,128)(2,1)} %pad.4.own_key_ref), custom_call_target="tpu_custom_call" | custom-call | tf_op jit(solution)/shard_map/attend/pallas_call | solution.py:486
  125.8 0.0 copy-done.1
  125.8 0.0 copy-start
  125.8 1.2 copy-done
  127.0 23.0 %output.1 = bf16[8,7168]{1,0:T(8,128)(2,1)S(1)} custom-call(bf16[16,64,512]{2,1,0:T(8,128)(2,1)S(1)} %copy-done, bf16[8,512,128]{2,1,0:T(8,128)(2,1)S(1)} %copy-done.1, bf16[1024,7168]{1,0:T(8,128)(2,1)} %wo_ref.1), custom_call_target="tpu_custom_call" | custom-call | tf_op jit(solution)/shard_map/output/pallas_call | solution.py:517
  150.0 0.7 reshape.11
  (1 shorter events, 0.0 us)
Async XLA Ops:
  0.0 125.8 %copy-start.1 = (bf16[8,512,128]{2,1,0:T(8,128)(2,1)S(1)}, bf16[8,512,128]{2,1,0:T(8,128)(2,1)}, u32[]{:S(2)}) copy-start(bf16[8,512,128]{2,1,0:T(8,128)(2,1)} %up_ref.1) | copy-start | bytes 3145732
  125.8 1.2 copy-start
